TPU v7x, 128 devices: a whole 4x4x4 slice. The times are simulated.
128 devices in a mesh: scene: 8 (over y, z_lo), frame: 16 (over x, z_hi, core).
Axes of the slice: x: 4, y: 4, z: 4 (z_hi: 2, z_lo: 2; z = z_hi * 2 + z_lo), core: 2. Of those that a mesh axis runs over, the one named last changes fastest.
Arguments:
- tokens: bfloat16 [16384, 1024], P(('scene', 'frame')), may hold values from -8 to 8
- covisible: int32 [8, 16, 16], P('scene'), may hold values 0 or 1
- w_query: bfloat16 [1024, 1024], replicated, may hold values from -0.1875 to 0.1875
- w_key: bfloat16 [1024, 1024], replicated, may hold values from -0.20625 to 0.20625
- w_value: bfloat16 [1024, 1024], replicated, may hold values from -0.1875 to 0.1875
- w_out: bfloat16 [1024, 1024], replicated, may hold values from -3 to 3
- cotangent: bfloat16 [16384, 1024], P(('scene', 'frame')), may hold values from -24 to 24
Outputs:
- result: bfloat16 [16384, 1024], P(('scene', 'frame'))
- grad_tokens: float32 [16384, 1024], P(('scene', 'frame'))
- grad_out_weight: float32 [1024, 1024], P('frame', 'scene')
All inputs are finite; a program needn't handle non-finite values. No bound on the sum of `covisible` on one device may be relied on, other than what follows from the above.
Results may differ from a plain program's by a relative error of at most 0.023.
Values may be sent and summed in bfloat16 or wider, within the bound.
No kernel may reach another device: no remote copies, remote signals or barrier semaphores. Data moves between devices by JAX's collectives and lax.ppermute only.
A program may use at most 128 MiB of HBM per device.

v0:
```python
import jax
import jax.numpy as jnp
from jax import lax
from jax.sharding import PartitionSpec as P

HEADS = 16
HEAD_DIM = 64


def shards(tokens, covisible, w_query, w_key, w_value, w_out, cotangent):
    row_count, feature_width = tokens.shape
    frame_count = lax.axis_size("frame")
    my_frame = lax.axis_index("frame")
    head_width = feature_width // HEADS
    score_scale = HEAD_DIM ** (-0.5)
    pair_table = covisible[0]
    frame_range = jnp.arange(frame_count, dtype=jnp.int32)
    own_mark = frame_range == my_frame
    seen_from = (lax.dynamic_index_in_dim(pair_table, my_frame, 0, keepdims=False) == 1) | own_mark
    queries = jnp.dot(tokens, w_query, preferred_element_type=jnp.float32).astype(jnp.bfloat16)
    key_rows = jnp.dot(tokens, w_key, preferred_element_type=jnp.float32).astype(jnp.bfloat16)
    value_rows = jnp.dot(tokens, w_value, preferred_element_type=jnp.float32).astype(jnp.bfloat16)
    all_keys, all_values = (
        lax.all_gather(key_rows, "frame", axis=0, tiled=True),
        lax.all_gather(value_rows, "frame", axis=0, tiled=True),
    )
    key_frames = all_keys.reshape(frame_count, row_count, HEADS, head_width)
    value_frames = all_values.reshape(frame_count, row_count, HEADS, head_width)
    query_heads = queries.reshape(row_count, HEADS, head_width)
    own_keys = lax.dynamic_index_in_dim(key_frames, my_frame, 0, keepdims=False)

    def frame_logits(key_panel, is_seen):
        logits = (
            jnp.einsum("qhd,khd->hqk", query_heads, key_panel, preferred_element_type=jnp.float32)
            * score_scale
        )
        return jnp.where(is_seen, logits, -1e30)

    start_top = jnp.max(frame_logits(own_keys, True), axis=2)
    start_total = jnp.zeros((HEADS, row_count), jnp.float32)

    def stats_step(carry, panels):
        key_panel, value_panel, is_seen = panels
        old_top, old_total = carry
        logits = frame_logits(key_panel, is_seen)
        new_top = jnp.maximum(old_top, jnp.max(logits, axis=2))
        new_total = old_total * jnp.exp(old_top - new_top) + jnp.sum(
            jnp.exp(logits - new_top[..., None]), axis=2
        )
        return ((new_top, new_total), None)

    (row_top, row_total), _ = lax.scan(
        stats_step, (start_top, start_total), (key_frames, value_frames, seen_from)
    )

    def chances_for(key_panel, is_seen):
        shifted = jnp.exp(frame_logits(key_panel, is_seen) - row_top[..., None])
        return (shifted / row_total[..., None]).astype(jnp.bfloat16)

    zero_panel = jnp.zeros((row_count, HEADS, head_width), jnp.float32)

    def attend_step(attended_sum, panels):
        key_panel, value_panel, is_seen = panels
        return (
            attended_sum
            + jnp.einsum(
                "hqk,khd->qhd",
                chances_for(key_panel, is_seen),
                value_panel,
                preferred_element_type=jnp.float32,
            ),
            None,
        )

    attended_full, _ = lax.scan(attend_step, zero_panel, (key_frames, value_frames, seen_from))
    attended = attended_full.reshape(row_count, feature_width).astype(jnp.bfloat16)
    result = jnp.dot(attended, w_out, preferred_element_type=jnp.float32).astype(jnp.bfloat16)
    grad_attended = jnp.dot(cotangent, w_out.T, preferred_element_type=jnp.float32).astype(
        jnp.bfloat16
    )
    grad_heads = grad_attended.reshape(row_count, HEADS, head_width)
    row_delta = jnp.sum(grad_heads.astype(jnp.float32) * attended_full, axis=2).T

    def logit_grads(key_panel, value_panel, is_seen):
        chances = chances_for(key_panel, is_seen)
        grad_chances = jnp.einsum(
            "qhd,khd->hqk", grad_heads, value_panel, preferred_element_type=jnp.float32
        )
        grad_logits = (
            chances.astype(jnp.float32) * (grad_chances - row_delta[..., None]) * score_scale
        ).astype(jnp.bfloat16)
        return (chances, grad_logits)

    def term_step(grad_sum, panels):
        key_panel, value_panel, is_seen = panels
        chances, grad_logits = logit_grads(key_panel, value_panel, is_seen)
        new_sum = grad_sum + jnp.einsum(
            "hqk,khd->qhd", grad_logits, key_panel, preferred_element_type=jnp.float32
        )
        key_term = jnp.einsum(
            "hqk,qhd->khd", grad_logits, query_heads, preferred_element_type=jnp.float32
        )
        value_term = jnp.einsum(
            "hqk,qhd->khd", chances, grad_heads, preferred_element_type=jnp.float32
        )
        return (new_sum, (key_term, value_term))

    grad_query_full, (key_terms, value_terms) = lax.scan(
        term_step, zero_panel, (key_frames, value_frames, seen_from)
    )
    grad_terms = jnp.concatenate(
        [
            key_terms.reshape(frame_count * row_count, feature_width),
            value_terms.reshape(frame_count * row_count, feature_width),
        ],
        axis=1,
    )
    summed = lax.psum_scatter(
        grad_terms.astype(jnp.bfloat16), "frame", scatter_dimension=0, tiled=True
    ).astype(jnp.float32)
    grad_key = summed[:, :feature_width].astype(jnp.bfloat16)
    grad_value = summed[:, feature_width:].astype(jnp.bfloat16)
    grad_query = grad_query_full.reshape(row_count, feature_width).astype(jnp.bfloat16)
    grad_tokens = jnp.dot(grad_query, w_query.T, preferred_element_type=jnp.float32)
    grad_tokens = grad_tokens + jnp.dot(grad_key, w_key.T, preferred_element_type=jnp.float32)
    grad_tokens = grad_tokens + jnp.dot(grad_value, w_value.T, preferred_element_type=jnp.float32)
    out_term = jnp.dot(attended.T, cotangent, preferred_element_type=jnp.float32)
    frame_part = lax.psum_scatter(
        out_term.astype(jnp.bfloat16), "frame", scatter_dimension=0, tiled=True
    )
    grad_out_weight = lax.psum_scatter(frame_part, "scene", scatter_dimension=1, tiled=True).astype(
        jnp.float32
    )
    return (result, grad_tokens, grad_out_weight)


def solution(mesh):
    in_specs = (
        P(("scene", "frame"), None),
        P("scene", None, None),
        P(),
        P(),
        P(),
        P(),
        P(("scene", "frame"), None),
    )
    out_specs = (P(("scene", "frame"), None), P(("scene", "frame"), None), P("frame", "scene"))
    return jax.shard_map(shards, mesh=mesh, in_specs=in_specs, out_specs=out_specs, check_vma=False)
```

profile of v0, /device:TPU:0, one launch (start us, length us, event | category | flops | bytes accessed | tf_op | source)
XLA Modules:
  0.0 524.5 jit_solution(12336230212077311401)
XLA Ops:
  7.2 3.0 convolution_convert_fusion.4
  10.3 2.8 convolution_convert_fusion.5
  17.3 51.7 %all-gather.5.cloned.1.call-done = bf16[2048,1024]{1,0:T(8,128)(2,1)} async-done(((bf16[128,1024]{1,0:T(8,128)(2,1)}), bf16[2048,1024]{1,0:T(8,128)(2,1)}) %all-gather.5.cloned.1.call-update) | async-done | bytes 4194320 | tf_op jit(solution)/shard_map/all_gather | solution.py:24
  69.0 6.5 %copy.44 = bf16[2048,1024]{0,1:T(8,128)(2,1)} copy(bf16[2048,1024]{1,0:T(8,128)(2,1)} %all-gather.5.cloned.1.call-done) | data formatting | bytes 8388608 | tf_op jit(solution)/shard_map/all_gather | solution.py:24
  75.5 3.6 copy.63
  79.7 3.1 copy.48
  83.2 43.4 %while.39 = (s32[]{:T(128)}, f32[16,128]{1,0:T(8,128)S(1)}, f32[16,128]{1,0:T(8,128)S(1)}, pred[16]{0:T(512)(128)(4,1)S(1)}, bf16[16,128,16,64]{1,3,2,0:T(8,128)...) while((s32[]{:T(128)}, f32[16,128]{1,0:T(8,128)S(1)}, ...), condition=%wide.region_4.5_spmd.clone, body=%wide.region_1.4_spmd.clone.sunk | while | flops 34871296 | bytes 2729061 | solution.py:52
  126.6 11.6 %reshape.50 = bf16[16,128,16,64]{3,2,1,0:T(8,128)(2,1)} reshape(bf16[2048,1024]{1,0:T(8,128)(2,1)} %all-gather.3.cloned.1.call-done) | data formatting | bytes 8388608 | tf_op jit(solution)/shard_map/reshape | solution.py:28
  138.3 10.3 %copy.47 = bf16[16,128,16,64]{1,3,2,0:T(8,128)(2,1)} copy(bf16[16,128,16,64]{3,2,1,0:T(8,128)(2,1)} %reshape.50) | data formatting | bytes 8388608
  148.5 61.8 %while.40 = (s32[]{:T(128)}, f32[128,16,64]{0,2,1:T(8,128)}, bf16[16,128,16,64]{1,3,2,0:T(8,128)(2,1)}, pred[16]{0:T(512)(128)(4,1)S(1)}, bf16[16,128,16,64]{1,3...) while((s32[]{:T(128)}, f32[128,16,64]{0,2,1:T(8,128)}, ...), condition=%wide.region_6.7_spmd.clone, body=%wide.region_5.6_spmd.clone.sunk | while | flops 68681728 | bytes 1853045 | solution.py:75
  149.1 3.1 fusion.110
  152.8 3.3 fusion.110
  156.7 3.3 fusion.110
  160.6 3.3 fusion.110
  164.4 3.3 fusion.110
  168.3 3.3 fusion.110
  172.2 3.3 fusion.110
  176.1 3.3 fusion.110
  179.9 3.3 fusion.110
  183.8 3.3 fusion.110
  187.7 3.3 fusion.110
  191.5 3.3 fusion.110
  195.4 3.3 fusion.110
  199.3 3.3 fusion.110
  203.2 3.3 fusion.110
  207.0 3.3 fusion.110
  214.0 136.8 %while.41 = (s32[]{:T(128)}, f32[128,16,64]{0,2,1:T(8,128)}, bf16[16,128,16,64]{1,3,2,0:T(8,128)(2,1)}, bf16[16,128,16,64]{1,3,2,0:T(8,128)(2,1)}, bf16[16,128,1...) while((s32[]{:T(128)}, f32[128,16,64]{0,2,1:T(8,128)}, ...), condition=%wide.region_9.10_spmd.clone, body=%wide.region_8.9_spmd.clone.sunk | while | flops 170655744 | bytes 7105685 | solution.py:108
  228.8 2.2 fusion.123
  245.9 2.2 fusion.123
  254.5 2.2 fusion.123
  263.0 2.2 fusion.123
  280.1 2.2 fusion.123
  288.7 2.2 fusion.123
  297.2 2.2 fusion.123
  314.4 2.2 fusion.123
  322.9 2.2 fusion.123
  331.4 2.2 fusion.123
  340.0 2.2 fusion.123
  350.8 5.7 %copy.52 = bf16[16,128,16,64]{1,0,3,2:T(8,128)(2,1)S(1)} copy(bf16[16,128,16,64]{1,3,2,0:T(8,128)(2,1)} %get-tuple-element.146) | data formatting | bytes 8388608 | tf_op jit(solution)/shard_map/convert.5
  356.5 5.7 %copy.53 = bf16[16,128,16,64]{1,0,3,2:T(8,128)(2,1)S(1)} copy(bf16[16,128,16,64]{1,3,2,0:T(8,128)(2,1)} %get-tuple-element.147) | data formatting | bytes 8388608 | tf_op jit(solution)/shard_map/convert.4
  362.2 6.6 %copy_bitcast_fusion = (bf16[2048,1024]{0,1:T(8,128)(2,1)}, bf16[2048,1024]{0,1:T(8,128)(2,1)}) fusion(bf16[128,8,16,128]{3,2,1,0:T(8,128)(2,1)S(1)} %bitcast.153, bf16[128,8,16,128]{3,2,1,0:T(8,128)(2,1)S(1)} %bitcast.152), kind=kLoop, calls=%fused_computation.56 | loop fusion | bytes 16777216 | tf_op jit(solution)/shard_map/reshape | solution.py:114
  370.8 8.3 %pad_maximum_fusion = bf16[2048,2048]{0,1:T(8,128)(2,1)} fusion(bf16[2048,1024]{0,1:T(8,128)(2,1)} %get-tuple-element.395, bf16[2048,1024]{0,1:T(8,128)(2,1)} %get-tuple-element.396), kind=kLoop, calls=%fused_computation.55 | loop fusion | flops 16777216 | bytes 16777216 | tf_op jit(solution)/shard_map/concatenate | solution.py:111
  379.2 12.3 %copy.54 = bf16[2048,2048]{1,0:T(8,128)(2,1)} copy(bf16[2048,2048]{0,1:T(8,128)(2,1)} %pad_maximum_fusion) | data formatting | bytes 16777216
  393.7 2.4 fusion.55
  396.2 10.6 %reduce-scatter.12.cloned.1.call-done = bf16[128,64]{1,0:T(8,128)(2,1)} async-done(((bf16[1024,64]{1,0:T(8,128)(2,1)}), bf16[128,64]{1,0:T(8,128)(2,1)}) %reduce-scatter.12.cloned.1.call-update) | async-done | bytes 16400
  408.3 104.4 %reduce-scatter.10.cloned.1.call-done = bf16[128,2048]{1,0:T(8,128)(2,1)} async-done(((bf16[2048,2048]{1,0:T(8,128)(2,1)}), bf16[128,2048]{1,0:T(8,128)(2,1)}) %reduce-scatter.10.cloned.1.call-update) | async-done | bytes 524304
  512.7 2.6 convolution_add_fusion.1
  515.3 2.6 convolution_add_fusion
  (238 shorter events, 178.5 us)
Async XLA Ops:
  7.2 8.4 %copy-start = (bf16[1024,1024]{1,0:T(8,128)(2,1)S(1)}, bf16[1024,1024]{1,0:T(8,128)(2,1)}, u32[]{:S(2)}) copy-start(bf16[1024,1024]{1,0:T(8,128)(2,1)} %param.18) | copy-start | bytes 6291460
  7.2 6.1 %copy-start.3 = (bf16[128,1024]{1,0:T(8,128)(2,1)S(1)}, bf16[128,1024]{1,0:T(8,128)(2,1)}, u32[]{:S(2)}) copy-start(bf16[128,1024]{1,0:T(8,128)(2,1)} %param.13) | copy-start | bytes 786436
  7.2 8.3 %copy-start.4 = (bf16[128,1024]{1,0:T(8,128)(2,1)S(1)}, bf16[128,1024]{1,0:T(8,128)(2,1)}, u32[]{:S(2)}) copy-start(bf16[128,1024]{1,0:T(8,128)(2,1)} %param.19) | copy-start | bytes 786436
  7.2 61.8 %all-gather.5.cloned.1.call-start = ((), (), s32[]{:S(2)}) async-start(), calls=%async_computation.4 | async-start | bytes 4456448 | tf_op jit(solution)/shard_map/all_gather | solution.py:24
  10.3 116.4 %all-gather.3.cloned.1.call-start = ((), (), s32[]{:S(2)}) async-start(), calls=%async_computation.3 | async-start | bytes 4456448 | tf_op jit(solution)/shard_map/all_gather | solution.py:25
  13.2 355.6 %reduce-scatter.8.cloned.1.call-start = ((), (), s32[]{:S(2)}) async-start(), calls=%async_computation.5 | async-start | bytes 2228224 | tf_op jit(solution)/shard_map/reduce_scatter | solution.py:128
  213.8 193.0 %reduce-scatter.12.cloned.1.call-start = ((), (), s32[]{:S(2)}) async-start(), calls=%async_computation.7 | async-start | bytes 294912
  370.5 142.1 %reduce-scatter.10.cloned.1.call-start = ((), (), s32[]{:S(2)}) async-start(), calls=%async_computation.6 | async-start | bytes 8912896
  391.5 1.0 copy-start.1
  512.7 2.7 copy-start.2
Sparse Core Ops, SparseCore 0:
  10.4 58.4 all-gather.4
  71.9 54.6 all-gather.2
  213.9 69.5 reduce-scatter.7
  370.7 36.0 reduce-scatter.11
  411.6 101.0 reduce-scatter.9
where the time goes:
time: 529 us; the launch traced here: 524 us
  matrix products  230 us (43%)
  waiting for transfers between devices  167 us (32%)
  local copies, waits for them, and re-layouts  98.2 us (19%)
  between operations  14 us (3%)
  other arithmetic  13.9 us (3%)
    unnamed x7, waiting for transfers between devices  115 us
    dot_general x33, matrix products, frame_logits(): jnp.einsum('qhd,khd->hqk', query_heads, key_panel, preferred_element_type...  63.6 us
    dot_general x16, matrix products, attend_step(): jnp.einsum('hqk,khd->qhd', chances_for(key_panel, is_seen), value_panel,...  52.4 us
    all_gather x1, waiting for transfers between devices, shards(): lax.all_gather(key_rows, 'frame', axis=0, tiled=True)  51.7 us
    dot_general x16, matrix products, term_step(): jnp.einsum('hqk,khd->qhd', grad_logits, key_panel, preferred_element_type...  35.3 us
    unnamed x16, local copies, waits for them, and re-layouts  32.9 us
    dynamic_slice x48, local copies, waits for them, and re-layouts, shards(): lax.scan(stats_step, (start_top, start_total), (key_frames, value_frames,...  28.2 us
    dot_general x16, matrix products, logit_grads(): jnp.einsum('qhd,khd->hqk', grad_heads, value_panel, preferred_element_typ...  21.5 us
  transfers between devices with their start and end apart: 5, of which 3 were waited for; matrix products, arithmetic and copies ran while one was open for 46% of the time, Pallas kernels for 0%

commit v1 on v0

v1 whole, which is shorter than its diff:
```python
import functools
import math

import jax
import jax.numpy as jnp
from jax import lax
from jax.experimental import pallas as pl
from jax.experimental.pallas import tpu as pltpu
from jax.sharding import PartitionSpec as P

HEAD_DIM = 64
BF = jnp.bfloat16
F32 = jnp.float32
HIDDEN = -1e30
NT = (((1,), (1,)), ((), ()))
VMEM = pl.BlockSpec(memory_space=pltpu.VMEM)
SMEM = pl.BlockSpec(memory_space=pltpu.SMEM)
ANY = pl.BlockSpec(memory_space=pl.ANY)
LOG2E = 1.0 / math.log(2.0)
SCALE = HEAD_DIM**-0.5


def dot(a, b):
    return jnp.dot(a, b, preferred_element_type=F32)


def dot_nt(a, b):
    return lax.dot_general(a, b, NT, preferred_element_type=F32)


def params(limit):
    return dict(
        compiler_params=pltpu.CompilerParams(vmem_limit_bytes=limit * 2**20),
        cost_estimate=pl.CostEstimate(flops=1, bytes_accessed=1, transcendentals=0),
    )


def start_all(pairs, arrived):
    copies = [pltpu.make_async_copy(src, dst, arrived.at[i]) for i, (src, dst) in enumerate(pairs)]
    for copy in copies:
        copy.start()
    return copies


def aligned(index, size):
    return pl.ds(pl.multiple_of(index * size, size), size)


def in_core_order(place, rows_ref, start, own, peer):
    rows = own.shape[0]
    core = place[2]
    rows_ref[pl.ds(pl.multiple_of(start + core * rows, rows), rows), :] = own[...]
    rows_ref[pl.ds(pl.multiple_of(start + (1 - core) * rows, rows), rows), :] = peer[...]


def fetch_kernel(place, wk, wv, wq, wo, columns, rows, pairs, arrived):
    z, core, block = place[1], place[2], place[3]
    chips = pairs.shape[1]
    wide = 2 * HEAD_DIM
    moves = [
        (w.at[:, pl.ds(pl.multiple_of(a * 2 * wide + z * wide, wide), wide)], pairs.at[slot, a])
        for slot, w in enumerate((wk, wv, wq))
        for a in range(chips)
    ]
    for a in range(chips):
        from_rows = aligned(chips * a + block, HEAD_DIM)
        moves.append((wo.at[from_rows, :], rows.at[a * HEAD_DIM : (a + 1) * HEAD_DIM, :]))
    copies = start_all(moves, arrived)

    def keep(slot, lanes):
        for a in range(0, chips, 2):
            both = jnp.concatenate([pairs[slot, a, :, lanes], pairs[slot, a + 1, :, lanes]], axis=1)
            columns[slot, :, a * HEAD_DIM : (a + 2) * HEAD_DIM] = both

    for slot in range(3):
        for a in range(chips):
            copies[slot * chips + a].wait()
        pl.when(core == 0)(functools.partial(keep, slot, slice(0, HEAD_DIM)))
        pl.when(core == 1)(functools.partial(keep, slot, slice(HEAD_DIM, wide)))
    for copy in copies[3 * chips :]:
        copy.wait()


def fetch(place, weights, chips):
    width = weights[0].shape[0]
    block = chips * HEAD_DIM
    return pl.pallas_call(
        fetch_kernel,
        in_specs=[SMEM] + [ANY] * 4,
        out_specs=[VMEM] * 2,
        out_shape=[jax.ShapeDtypeStruct((3, width, block), BF), jax.ShapeDtypeStruct((block, width), BF)],
        scratch_shapes=[
            pltpu.VMEM((3, chips, width, 2 * HEAD_DIM), BF),
            pltpu.SemaphoreType.DMA((4 * chips,)),
        ],
        name="fetch",
        **params(48),
    )(place, *weights)


def project_kernel(place, own, peer, cot, peer_cot, held, held_out, *rest):
    outs, (tok, grads, turned) = rest[:-3], rest[-3:]
    in_core_order(place, tok, 0, own, peer)
    in_core_order(place, grads, 0, cot, peer_cot)
    for slot in range(3):
        part = dot(tok[...], held[slot])
        if slot == 2:
            part = part * (SCALE * LOG2E)
        turned[slot] = part.astype(BF).T
    turned[3] = dot_nt(held_out[...], grads[...]).astype(BF)
    for d, out in enumerate(outs):
        head = lax.rem(place[0] + d, len(outs))
        for slot in range(4):
            out[slot * HEAD_DIM : (slot + 1) * HEAD_DIM, :] = turned[slot, aligned(head, HEAD_DIM), :]


def project(place, tokens, cotangents, weights, chips):
    rows, width = tokens[0].shape
    block = chips * HEAD_DIM
    return pl.pallas_call(
        project_kernel,
        in_specs=[SMEM] + [VMEM] * 6,
        out_specs=[VMEM] * chips,
        out_shape=[jax.ShapeDtypeStruct((4 * HEAD_DIM, 2 * rows), BF)] * chips,
        scratch_shapes=[
            pltpu.VMEM((2 * rows, width), BF),
            pltpu.VMEM((2 * rows, width), BF),
            pltpu.VMEM((4, block, 2 * rows), BF),
        ],
        name="project",
        **params(16),
    )(place, *tokens, *cotangents, *weights)


def frame_at(place, chips, slot, core):
    plane, d = slot // chips, slot % chips
    x = lax.rem(place[0] + chips - d, chips)
    z = lax.rem(place[1] + plane, 2)
    return x * 4 + z * 2 + core


def attend_kernel(chips, step, chunk, place, cov, *rest):
    slots = 2 * chips
    parts, outs, rest = rest[:slots], rest[slots : slots + chips], rest[slots + chips :]
    packed, keys, even, odd, raw_even, raw_odd, att, grad_query, total = rest
    rows = slots * step
    frame_rows = step // 2
    frames = 2 * slots
    lane = lax.broadcasted_iota(jnp.int32, (step, 128), 1)
    half = lax.broadcasted_iota(jnp.int32, (step, 128), 0) // frame_rows
    ones = (lane >= frames) & (lane < frames + 3)
    for slot, part in enumerate(parts):
        at = slot * step
        packed[:, at : at + step] = part[...]
        keys[at : at + step, 0:128] = part[0:128, :].T
        keys[at : at + step, 128:256] = jnp.where((lane == half + 2 * slot) | ones, 1.0, 0.0).astype(BF)
    total[...] = jnp.zeros_like(total)
    chunks = range(0, rows, chunk)
    bias_row = lax.broadcasted_iota(jnp.int32, (frames, frame_rows), 0)
    delta_row = lax.broadcasted_iota(jnp.int32, (16, step), 0)
    rest_rows = jnp.zeros((128 - frames, step), BF)
    last_rows = jnp.zeros((112 - frames, step), BF)
    frame_zeros = jnp.zeros((frames, step), BF)
    sum_rows = jnp.ones((16, chunk), BF)
    zero = jnp.zeros((HEAD_DIM, step), F32)
    none = jnp.zeros((HEAD_DIM, step), BF)

    def columns(ref, first, i):
        return ref[first : first + HEAD_DIM, pl.ds(pl.multiple_of(i * step, step), step)]

    def score_side(i):
        biases = []
        for core in range(2):
            query_frame = frame_at(place, chips, i, core)
            bias = jnp.zeros((frames, frame_rows), F32)
            for key in range(frames):
                key_frame = frame_at(place, chips, key // 2, key % 2)
                seen = jnp.logical_or(cov[0, query_frame, key_frame] == 1, query_frame == key_frame)
                bias = jnp.where(bias_row == key, jnp.where(seen, 0.0, HIDDEN), bias)
            biases.append(bias)
        bias = jnp.concatenate(biases, axis=1).astype(BF)
        return jnp.concatenate([columns(packed, 128, i), none, bias, rest_rows], axis=0)

    def grad_sides(i, inverse, delta):
        grad = columns(packed, 192, i)
        high = delta.astype(BF).astype(F32)
        middle = (delta - high).astype(BF).astype(F32)
        low = delta - high - middle
        deltas = jnp.where(
            delta_row == 0, -high, jnp.where(delta_row == 1, -middle, jnp.where(delta_row == 2, -low, 0.0))
        ).astype(BF)
        query = columns(packed, 128, i).astype(F32) * (inverse * (1.0 / LOG2E))
        back = jnp.concatenate(
            [
                jnp.concatenate([zero, grad.astype(F32) * inverse], axis=0).astype(BF).T,
                jnp.concatenate([query, zero], axis=0).astype(BF).T,
            ],
            axis=0,
        )
        return jnp.concatenate([none, grad, frame_zeros, deltas, last_rows], axis=0), back

    def together(score=None, weigh=None, grad=None):
        if score:
            at_score, logits_to = score
            score_right = score_side(at_score)
            top = jnp.full((8, step), HIDDEN, F32)
        if weigh:
            at_weigh, logits_from, weigh_top, raw_to = weigh
            summed = jnp.zeros((HEAD_DIM + 16, step), F32)
        if grad:
            at_grad, raw_from, inverse, delta = grad
            grad_right, back = grad_sides(at_grad, inverse, delta)
            query_sum = zero
        for c in chunks:
            here = slice(c, c + chunk)
            if score:
                part = dot(keys[here, :], score_right)
                logits_to[here, :] = part
                top = jnp.maximum(top, jnp.max(part.reshape(chunk // 8, 8, step), axis=0))
            if weigh:
                raw = jnp.exp2(logits_from[here, :] - weigh_top).astype(BF)
                raw_to[here, :] = raw
                summed = summed + dot(jnp.concatenate([packed[HEAD_DIM:128, here], sum_rows], axis=0), raw)
            if grad:
                raw = raw_from[here, :]
                change = raw * dot(keys[here, :], grad_right).astype(BF)
                query_sum = query_sum + dot(packed[0:HEAD_DIM, here], change)
                total[here, :] += dot(jnp.concatenate([raw, change], axis=1), back)
        if grad:
            at = pl.ds(pl.multiple_of(at_grad * step, step), step)
            grad_query[:, at] = (query_sum * (inverse * SCALE)).astype(BF)
        got = ()
        if score:
            got += (jnp.max(top, axis=0, keepdims=True),)
        if weigh:
            inverse = 1.0 / summed[HEAD_DIM : HEAD_DIM + 1, :]
            attended = summed[0:HEAD_DIM, :] * inverse
            att[:, pl.ds(pl.multiple_of(at_weigh * step, step), step)] = attended.astype(BF)
            delta = jnp.sum(columns(packed, 192, at_weigh).astype(F32) * attended, axis=0, keepdims=True)
            got += (inverse, delta)
        return got

    (top,) = together(score=(0, even))
    carry = together(score=(1, odd), weigh=(0, even, top, raw_even))

    def body(j, carry):
        i = 2 * j + 1
        top, inverse, delta = carry
        top, inverse, delta = together((i + 1, even), (i, odd, top, raw_odd), (i - 1, raw_even, inverse, delta))
        return together((i + 2, odd), (i + 1, even, top, raw_even), (i, raw_odd, inverse, delta))

    top, inverse, delta = lax.fori_loop(0, slots // 2 - 1, body, carry)
    inverse, delta = together(
        weigh=(slots - 1, odd, top, raw_odd), grad=(slots - 2, raw_even, inverse, delta)
    )
    together(grad=(slots - 1, raw_odd, inverse, delta))
    for slot in range(slots):
        here = slice(slot * step, (slot + 1) * step)
        there = slice(slot // chips * step, (slot // chips + 1) * step)
        out = outs[slot % chips]
        out[0:HEAD_DIM, there] = grad_query[:, here]
        out[HEAD_DIM : 3 * HEAD_DIM, there] = total[here, :].astype(BF).T
        out[3 * HEAD_DIM : 4 * HEAD_DIM, there] = att[:, here]


def attend(place, pairs, parts, chips):
    step = parts[0].shape[1]
    slots = 2 * chips
    rows = slots * step
    return pl.pallas_call(
        functools.partial(attend_kernel, chips, step, 1024),
        in_specs=[SMEM, SMEM] + [VMEM] * slots,
        out_specs=[VMEM] * chips,
        out_shape=[jax.ShapeDtypeStruct((4 * HEAD_DIM, 2 * step), BF)] * chips,
        scratch_shapes=[
            pltpu.VMEM((4 * HEAD_DIM, rows), BF),
            pltpu.VMEM((rows, 256), BF),
            pltpu.VMEM((rows, step), F32),
            pltpu.VMEM((rows, step), F32),
            pltpu.VMEM((rows, step), BF),
            pltpu.VMEM((rows, step), BF),
            pltpu.VMEM((HEAD_DIM, rows), BF),
            pltpu.VMEM((HEAD_DIM, rows), BF),
            pltpu.VMEM((rows, 128), F32),
        ],
        name="attend",
        **params(40),
    )(place, pairs, *parts)


def finish_kernel(place, held, held_out, *rest):
    parts, (near, far, send, turned, wide) = rest[:-5], rest[-5:]
    chips = len(parts)
    rows, width = near.shape[0], held.shape[1]
    core = place[2]
    for d, part in enumerate(parts):
        head = lax.rem(place[0] + d, chips)
        for slot in range(4):
            turned[slot, aligned(head, HEAD_DIM), :] = part[slot * HEAD_DIM : (slot + 1) * HEAD_DIM, :]
    terms = None
    for slot, weight in enumerate((2, 0, 1)):
        term = dot_nt(turned[slot].T, held[weight])
        terms = term if terms is None else terms + term
    wide[:, 0:width] = terms
    wide[:, width : 2 * width] = dot(turned[3].T, held_out[...])
    near[...] = wide[aligned(core, rows), :]
    far[...] = wide[aligned(2 + core, rows), :]
    send[0:rows, :] = wide[aligned(1 - core, rows), :].astype(BF)
    send[rows : 2 * rows, :] = wide[aligned(3 - core, rows), :].astype(BF)


def finish(place, parts, weights):
    chips = len(parts)
    rows, width = parts[0].shape[1] // 4, weights[0].shape[1]
    block = chips * HEAD_DIM
    keep = jax.ShapeDtypeStruct((rows, 2 * width), F32)
    return pl.pallas_call(
        finish_kernel,
        in_specs=[SMEM] + [VMEM] * (2 + chips),
        out_specs=[VMEM] * 3,
        out_shape=[keep, keep, jax.ShapeDtypeStruct((2 * rows, 2 * width), BF)],
        scratch_shapes=[pltpu.VMEM((4, block, 4 * rows), BF), pltpu.VMEM((4 * rows, 2 * width), F32)],
        name="finish",
        **params(24),
    )(place, *weights, *parts)


def out_terms_kernel(place, *rest):
    parts, cots, rest = rest[0:4], rest[4:8], rest[8:]
    outs, (turned, cot, wide) = rest[:-3], rest[-3:]
    rows = cots[0].shape[0]
    in_core_order(place, cot, 0, cots[0], cots[1])
    in_core_order(place, cot, 2 * rows, cots[2], cots[3])
    for d, part in enumerate(parts):
        turned[aligned(lax.rem(place[0] + d, len(parts)), HEAD_DIM), :] = part[3 * HEAD_DIM : 4 * HEAD_DIM, :]
    wide[...] = dot(turned[...], cot[...])
    for d, out in enumerate(outs):
        out[...] = wide[:, aligned(lax.rem(place[4] + d, len(outs)), out.shape[1])].astype(BF)


def out_terms(place, parts, cotangents, cuts):
    chips = len(parts)
    rows, width = cotangents[0].shape
    block = chips * HEAD_DIM
    return pl.pallas_call(
        out_terms_kernel,
        in_specs=[SMEM] + [VMEM] * (chips + 4),
        out_specs=[VMEM] * cuts,
        out_shape=[jax.ShapeDtypeStruct((block, width // cuts), BF)] * cuts,
        scratch_shapes=[
            pltpu.VMEM((block, 4 * rows), BF),
            pltpu.VMEM((4 * rows, width), BF),
            pltpu.VMEM((block, width), F32),
        ],
        name="out_terms",
        **params(16),
    )(place, *parts, *cotangents)


def added(parts):
    total = parts[0][...].astype(F32)
    for part in parts[1:]:
        total = total + part[...].astype(F32)
    return total


def sum_heads_kernel(chips, place, *rest):
    parts, outs, wide = rest[: -1 - chips], rest[-1 - chips : -1], rest[-1]
    wide[...] = added(parts)
    for d, out in enumerate(outs):
        out[...] = wide[aligned(lax.rem(place[0] + d, chips), HEAD_DIM), :].astype(out.dtype)


def sum_heads(place, parts):
    rows, lanes = parts[0].shape
    chips = rows // HEAD_DIM
    return pl.pallas_call(
        functools.partial(sum_heads_kernel, chips),
        in_specs=[SMEM] + [VMEM] * len(parts),
        out_specs=[VMEM] * chips,
        out_shape=[jax.ShapeDtypeStruct((HEAD_DIM, lanes), F32 if d == 0 else BF) for d in range(chips)],
        scratch_shapes=[pltpu.VMEM((rows, lanes), F32)],
        name="sum_heads",
        **params(16),
    )(place, *parts)


def sum_columns_kernel(place, *rest):
    parts, (keep, send, wide) = rest[:-3], rest[-3:]
    wide[...] = added(parts)
    lanes = keep.shape[1]
    keep[...] = wide[:, aligned(place[5], lanes)]
    send[...] = wide[:, aligned(1 - place[5], lanes)].astype(BF)


def sum_columns(place, parts):
    rows, lanes = parts[0].shape
    return pl.pallas_call(
        sum_columns_kernel,
        in_specs=[SMEM] + [VMEM] * len(parts),
        out_specs=[VMEM] * 2,
        out_shape=[jax.ShapeDtypeStruct((rows, lanes // 2), F32), jax.ShapeDtypeStruct((rows, lanes // 2), BF)],
        scratch_shapes=[pltpu.VMEM((rows, lanes), F32)],
        name="sum_columns",
        **params(16),
    )(place, *parts)


def shifted(parts, axis, sign):
    size = len(parts)
    return [parts[0]] + [
        lax.ppermute(parts[d], axis, [(i, (i + sign * d) % size) for i in range(size)]) for d in range(1, size)
    ]


def shards(tokens, covisible, w_query, w_key, w_value, w_out, cotangent):
    chips = lax.axis_size("fx")
    assert chips == 4
    swap = [(0, 1), (1, 0)]
    x, z, core, y, low = (lax.axis_index(name) for name in ("fx", "fz", "fc", "sy", "sl"))
    place = jnp.stack([x, z, core, z * 2 + core, y, low]).astype(jnp.int32)

    def across(part, axis):
        return lax.ppermute(part, axis, swap)

    weights = fetch(place, (w_key, w_value, w_query, w_out), chips)
    far_tokens, far_cotangent = across(tokens, "fz"), across(cotangent, "fz")
    peer_tokens, peer_cotangent = across(tokens, "fc"), across(cotangent, "fc")
    near = shifted(project(place, (tokens, peer_tokens), (cotangent, peer_cotangent), weights, chips), "fx", 1)
    near[1], far_tokens, far_cotangent = lax.optimization_barrier((near[1], far_tokens, far_cotangent))
    far_peer_tokens, far_peer_cotangent = across(far_tokens, "fc"), across(far_cotangent, "fc")
    far = shifted(
        project(place, (far_tokens, far_peer_tokens), (far_cotangent, far_peer_cotangent), weights, chips), "fx", 1
    )

    terms = shifted(attend(place, covisible, near + far, chips), "fx", -1)

    cotangents = (cotangent, peer_cotangent, far_cotangent, far_peer_cotangent)
    cuts = out_terms(place, terms, cotangents, lax.axis_size("sy"))
    terms, cuts = lax.optimization_barrier((terms, cuts))
    cuts = shifted(cuts, "sy", 1)
    own, far_own, away = finish(place, terms, weights)
    sent, cuts = lax.optimization_barrier((across(away, "fc"), cuts))
    rows, width = tokens.shape
    far_sum = (far_own + sent[rows:].astype(F32)).astype(BF)
    cuts, _ = lax.optimization_barrier((cuts, far_sum))
    far_sum = across(far_sum, "fz")
    tiles = shifted(sum_heads(place, cuts), "fx", 1)
    tile, other = sum_columns(place, tiles)
    grad_out_weight = tile + across(other, "sl").astype(F32)
    grad_tokens, result = (
        own[:, part] + sent[:rows, part].astype(F32) + far_sum[:, part].astype(F32)
        for part in (slice(0, width), slice(width, 2 * width))
    )
    return (result.astype(BF), grad_tokens, grad_out_weight)


def solution(mesh):
    names = ("sy", "sl", "fx", "fz", "fc")
    split = jax.sharding.Mesh(mesh.devices.reshape(-1, 2, 4, 2, 2), names)
    rows = P(names, None)
    in_specs = (rows, P(names[:2], None, None), P(), P(), P(), P(), rows)
    out_specs = (rows, rows, P(names[2:], names[:2]))
    return jax.shard_map(shards, mesh=split, in_specs=in_specs, out_specs=out_specs, check_vma=False)
```

time: 529 us -> 98 us (0.19)
  matrix products: 230 us -> 0 us
  waiting for transfers between devices: 167 us -> 36.5 us
  local copies, waits for them, and re-layouts: 98.2 us -> 1.69 us
  starting transfers between devices: 0.61 us -> 32.8 us
  Pallas kernels: 0 us -> 24.3 us
  between operations: 14 us -> 0.78 us
  other arithmetic: 13.9 us -> 1.84 us
    dot_general x122 -> x0, matrix products: 230 us -> none  [the longest x33 63.6 us: frame_logits(): jnp.einsum('qhd,khd->hqk', query_heads, key_panel, preferred_element_type...]
    unnamed x7 -> x0, waiting for transfers between devices: 115 us -> none
    all_gather x2 -> x0, waiting for transfers between devices: 51.8 us -> none  [the longest x1 51.7 us: shards(): lax.all_gather(key_rows, 'frame', axis=0, tiled=True)]
    ppermute x0 -> x24, waiting for transfers between devices: none -> 36.5 us  [the longest x15 27.4 us: shifted(): lax.ppermute(parts[d], axis, [(i, (i + sign * d) % size) for i in range(s...]
    ppermute x0 -> x24, starting transfers between devices: none -> 32.8 us  [the longest x15 23.2 us: shifted(): lax.ppermute(parts[d], axis, [(i, (i + sign * d) % size) for i in range(s...]
    unnamed x16 -> x8, local copies, waits for them, and re-layouts: 32.9 us -> 1.61 us
    dynamic_slice x49 -> x0, local copies, waits for them, and re-layouts: 28.8 us -> none  [the longest x48 28.2 us: shards(): lax.scan(stats_step, (start_top, start_total), (key_frames, value_frames,...]
    pallas_call x0 -> x8, Pallas kernels: none -> 24.3 us  [the longest x1 14.3 us: attend(): pl.pallas_call(functools.partial(attend_kernel, chips, step, 1024), in_sp...]
  transfers between devices with their start and end apart: 5 -> 24, of which waited for: 3 -> 12; matrix products, arithmetic and copies ran while one was open for 46% -> 1% of each run, Pallas kernels for 0% -> 7%
where the time goes in v1:
time: 98 us; the launch traced here: 97.9 us
  waiting for transfers between devices  36.5 us (37%)
  starting transfers between devices  32.8 us (33%)
  Pallas kernels  24.3 us (25%)
  other arithmetic  1.84 us (2%)
  local copies, waits for them, and re-layouts  1.69 us (2%)
    ppermute x15, waiting for transfers between devices, shifted(): lax.ppermute(parts[d], axis, [(i, (i + sign * d) % size) for i in range(s...  27.4 us
    ppermute x15, starting transfers between devices, shifted(): lax.ppermute(parts[d], axis, [(i, (i + sign * d) % size) for i in range(s...  23.2 us
    pallas_call x1, Pallas kernels, attend(): pl.pallas_call(functools.partial(attend_kernel, chips, step, 1024), in_sp...  14.3 us
    ppermute x9, starting transfers between devices, across(): return lax.ppermute(part, axis, swap)  9.61 us
    ppermute x9, waiting for transfers between devices, across(): return lax.ppermute(part, axis, swap)  9.07 us
    pallas_call x2, Pallas kernels, project(): pl.pallas_call(project_kernel, in_specs=[SMEM] + [VMEM] * 6, out_specs=[V...  2.74 us
    pallas_call x1, Pallas kernels, fetch(): pl.pallas_call(fetch_kernel, in_specs=[SMEM] + [ANY] * 4, out_specs=[VMEM...  2.73 us
    pallas_call x1, Pallas kernels, finish(): pl.pallas_call(finish_kernel, in_specs=[SMEM] + [VMEM] * (2 + chips), out...  2.13 us
  transfers between devices with their start and end apart: 24, of which 12 were waited for; matrix products, arithmetic and copies ran while one was open for 1% of the time, Pallas kernels for 7%

profile of v1, /device:TPU:0, one launch (start us, length us, event | category | flops | bytes accessed | tf_op | source)
XLA Modules:
  0.0 97.9 jit_solution(4093491695004233815)
XLA Ops:
  0.6 0.1 collective-permute-start
  0.7 0.5 collective-permute-start.1
  1.2 4.0 %collective-permute-start.3 = (bf16[128,1024]{1,0:T(8,128)(2,1)}, bf16[128,1024]{1,0:T(8,128)(2,1)S(1)}, u32[]{:S(2)}, u32[]{:S(2)}) collective-permute-start(bf16[128,1024]{1,0:T(8,128)(2,1)} %own.1), channel_id=1, source_target_pairs={{0,2},{2,0},{1,3},{3,1},{4,6},{6,4},{5,7},{7,5},{8,10},{10,8},{9,1... | collective-permute-start | bytes 786440 | tf_op jit(solution)/shard_map/ppermute | solution.py:424
  5.2 0.0 collective-permute-start.4
  5.2 0.1 stack.27.place
  5.3 1.6 %copy-done = bf16[1024,1024]{1,0:T(8,128)(2,1)S(1)} copy-done((bf16[1024,1024]{1,0:T(8,128)(2,1)S(1)}, bf16[1024,1024]{1,0:T(8,128)(2,1)}, u32[]{:S(2)}) %copy-start) | copy-done | bytes 2097176
  6.9 2.7 %fetch.1 = (bf16[3,1024,256]{2,1,0:T(8,128)(2,1)S(1)}, bf16[256,1024]{1,0:T(8,128)(2,1)S(1)}) custom-call(s32[6]{0:T(128)S(1)} %stack.27.place, bf16[1024,1024]{1,0:T(8,128)(2,1)S(1)} %copy-done, bf16[1024,1024]{1,0:T(8,128)(2,1)} %wv.1, bf16[1024,1024]{1,0:T(8,128)(2,1)} %wq.1, bf16[1024,1024]{1,0:T(8,128)(2,1)} %wo.1), custom_call_target="tpu_custom_call" | custom-call | flops 1 | bytes 1 | tf_op jit(solution)/shard_map/fetch/pallas_call | solution.py:87
  9.7 1.4 %project.2 = (bf16[256,256]{1,0:T(8,128)(2,1)S(1)}, bf16[256,256]{1,0:T(8,128)(2,1)S(1)}, bf16[256,256]{1,0:T(8,128)(2,1)S(1)}, bf16[256,256]{1,0:T(8,128)(2,1)S(1)}) custom-call(s32[6]{0:T(128)S(1)} %stack.27.place, bf16[128,1024]{1,0:T(8,128)(2,1)S(1)} %copy-done.2, bf16[128,1024]{1,0:T(8,128)(2,1)S(1)} %collective-permute-done.peer, ...), custom_call_target="tpu_custom_call" | custom-call | flops 1 | bytes 1 | tf_op jit(solution)/shard_map/project/pallas_call | solution.py:120
  11.1 1.6 %collective-permute-start.2 = (bf16[256,256]{1,0:T(8,128)(2,1)S(1)}, bf16[256,256]{1,0:T(8,128)(2,1)S(1)}, u32[]{:S(2)}, u32[]{:S(2)}) collective-permute-start(bf16[256,256]{1,0:T(8,128)(2,1)S(1)} %get-tuple-element.53), channel_id=1, source_target_pairs={{0,4},{4,8},{8,12},{12,0},{1,5},{5,9},{9,13},{13,1},{2,6},{6,10},{... | collective-permute-start | bytes 393224 | tf_op jit(solution)/shard_map/ppermute | solution.py:412
  12.6 4.9 %collective-permute-done.4.cot.rest_6_ = bf16[128,1024]{1,0:T(8,128)(2,1)S(1)} collective-permute-done((bf16[128,1024]{1,0:T(8,128)(2,1)}, bf16[128,1024]{1,0:T(8,128)(2,1)S(1)}, u32[]{:S(2)}, u32[]{:S(2)}) %collective-permute-start.4) | collective-permute-done | bytes 262176 | tf_op jit(solution)/shard_map/ppermute | solution.py:424
  17.6 0.5 collective-permute-start.8
  18.1 3.0 %collective-permute-start.5 = (bf16[256,256]{1,0:T(8,128)(2,1)S(1)}, bf16[256,256]{1,0:T(8,128)(2,1)S(1)}, u32[]{:S(2)}, u32[]{:S(2)}) collective-permute-start(bf16[256,256]{1,0:T(8,128)(2,1)S(1)} %get-tuple-element.55), channel_id=1, source_target_pairs={{0,8},{4,12},{8,0},{12,4},{1,9},{5,13},{9,1},{13,5},{2,10},{6,14},... | collective-permute-start | bytes 393224 | tf_op jit(solution)/shard_map/ppermute | solution.py:412
  21.1 1.1 %collective-permute-start.6 = (bf16[256,256]{1,0:T(8,128)(2,1)S(1)}, bf16[256,256]{1,0:T(8,128)(2,1)S(1)}, u32[]{:S(2)}, u32[]{:S(2)}) collective-permute-start(bf16[256,256]{1,0:T(8,128)(2,1)S(1)} %get-tuple-element.56), channel_id=1, source_target_pairs={{0,12},{4,0},{8,4},{12,8},{1,13},{5,1},{9,5},{13,9},{2,14},{6,2},{... | collective-permute-start | bytes 393224 | tf_op jit(solution)/shard_map/ppermute | solution.py:412
  22.3 1.4 %project.3 = (bf16[256,256]{1,0:T(8,128)(2,1)S(1)}, bf16[256,256]{1,0:T(8,128)(2,1)S(1)}, bf16[256,256]{1,0:T(8,128)(2,1)S(1)}, bf16[256,256]{1,0:T(8,128)(2,1)S(1)}) custom-call(s32[6]{0:T(128)S(1)} %stack.27.place, bf16[128,1024]{1,0:T(8,128)(2,1)S(1)} %collective-permute-done.3.own, bf16[128,1024]{1,0:T(8,128)(2,1)S(1)} %collective-permute-done.7.peer, ...), custom_call_target="tpu_custom_call" | custom-call | flops 1 | bytes 1 | tf_op jit(solution)/shard_map/project/pallas_call | solution.py:120
  23.6 1.0 collective-permute-start.9
  24.6 0.7 collective-permute-start.10
  25.3 2.5 %collective-permute-start.11 = (bf16[256,256]{1,0:T(8,128)(2,1)S(1)}, bf16[256,256]{1,0:T(8,128)(2,1)S(1)}, u32[]{:S(2)}, u32[]{:S(2)}) collective-permute-start(bf16[256,256]{1,0:T(8,128)(2,1)S(1)} %get-tuple-element.62), channel_id=1, source_target_pairs={{0,12},{4,0},{8,4},{12,8},{1,13},{5,1},{9,5},{13,9},{2,14},{6,2},{... | collective-permute-start | bytes 393224 | tf_op jit(solution)/shard_map/ppermute | solution.py:412
  27.9 0.3 collective-permute-done.6.rest_3_
  28.2 4.4 %collective-permute-done.9.rest_5_ = bf16[256,256]{1,0:T(8,128)(2,1)S(1)} collective-permute-done((bf16[256,256]{1,0:T(8,128)(2,1)S(1)}, bf16[256,256]{1,0:T(8,128)(2,1)S(1)}, u32[]{:S(2)}, u32[]{:S(2)}) %collective-permute-start.9) | collective-permute-done | bytes 131104 | tf_op jit(solution)/shard_map/ppermute | solution.py:412
  32.6 1.0 collective-permute-done.11.rest_7_
  33.6 14.3 %attend.1 = (bf16[256,512]{1,0:T(8,128)(2,1)S(1)}, bf16[256,512]{1,0:T(8,128)(2,1)S(1)}, bf16[256,512]{1,0:T(8,128)(2,1)S(1)}, bf16[256,512]{1,0:T(8,128)(2,1)S(1)}) custom-call(s32[6]{0:T(128)S(1)} %stack.27.place, s32[1,16,16]{2,1,0:T(8,128)S(1)} %copy-done.3, bf16[256,256]{1,0:T(8,128)(2,1)S(1)} %get-tuple-element.52.rest_0_, ...), custom_call_target="tpu_custom_call" | custom-call | flops 1 | bytes 1 | tf_op jit(solution)/shard_map/attend/pallas_call | solution.py:270
  47.8 2.7 %collective-permute-start.12 = (bf16[256,512]{1,0:T(8,128)(2,1)S(1)}, bf16[256,512]{1,0:T(8,128)(2,1)S(1)}, u32[]{:S(2)}, u32[]{:S(2)}) collective-permute-start(bf16[256,512]{1,0:T(8,128)(2,1)S(1)} %get-tuple-element.64), channel_id=1, source_target_pairs={{0,12},{4,0},{8,4},{12,8},{1,13},{5,1},{9,5},{13,9},{2,14},{6,2},{... | collective-permute-start | bytes 786440 | tf_op jit(solution)/shard_map/ppermute | solution.py:412
  50.5 0.8 collective-permute-start.13
  51.3 0.2 collective-permute-start.14
  51.5 10.1 %collective-permute-done.12.rest_1_ = bf16[256,512]{1,0:T(8,128)(2,1)S(1)} collective-permute-done((bf16[256,512]{1,0:T(8,128)(2,1)S(1)}, bf16[256,512]{1,0:T(8,128)(2,1)S(1)}, u32[]{:S(2)}, u32[]{:S(2)}) %collective-permute-start.12) | collective-permute-done | bytes 262176 | tf_op jit(solution)/shard_map/ppermute | solution.py:412
  61.6 3.7 %collective-permute-done.14.rest_3_ = bf16[256,512]{1,0:T(8,128)(2,1)S(1)} collective-permute-done((bf16[256,512]{1,0:T(8,128)(2,1)S(1)}, bf16[256,512]{1,0:T(8,128)(2,1)S(1)}, u32[]{:S(2)}, u32[]{:S(2)}) %collective-permute-start.14) | collective-permute-done | bytes 262176 | tf_op jit(solution)/shard_map/ppermute | solution.py:412
  65.3 1.2 %out_terms.1 = (bf16[256,256]{1,0:T(8,128)(2,1)S(1)}, bf16[256,256]{1,0:T(8,128)(2,1)S(1)}, bf16[256,256]{1,0:T(8,128)(2,1)S(1)}, bf16[256,256]{1,0:T(8,128)(2,1)S(1)}) custom-call(s32[6]{0:T(128)S(1)} %stack.27.place, bf16[256,512]{1,0:T(8,128)(2,1)S(1)} %get-tuple-element.71.rest_0_, bf16[256,512]{1,0:T(8,128)(2,1)S(1)} %collective-permute-done.12.rest_1_, ...), custom_call_target="tpu_custom_call" | custom-call | flops 1 | bytes 1 | tf_op jit(solution)/shard_map/out_terms/pallas_call | solution.py:345
  66.5 2.1 %finish.1 = (f32[128,2048]{1,0:T(8,128)S(1)}, f32[128,2048]{1,0:T(8,128)S(1)}, bf16[256,2048]{1,0:T(8,128)(2,1)S(1)}) custom-call(s32[6]{0:T(128)S(1)} %stack.27.place, bf16[3,1024,256]{2,1,0:T(8,128)(2,1)S(1)} %get-tuple-element.50.held, bf16[256,1024]{1,0:T(8,128)(2,1)S(1)} %get-tuple-element.51.held_out, bf16[256,512]{1,0:T(8,128)(2,1)S(1)} %get-tuple-element.71.rest_0_, ...), custom_call_target="tpu_custom_call" | custom-call | flops 1 | bytes 1 | tf_op jit(solution)/shard_map/finish/pallas_call | solution.py:317
  68.6 0.1 collective-permute-start.15
  68.7 1.6 %collective-permute-start.16 = (bf16[256,256]{1,0:T(8,128)(2,1)S(1)}, bf16[256,256]{1,0:T(8,128)(2,1)S(1)}, u32[]{:S(2)}, u32[]{:S(2)}) collective-permute-start(bf16[256,256]{1,0:T(8,128)(2,1)S(1)} %get-tuple-element.78), channel_id=1, source_target_pairs={{0,32},{32,64},{64,96},{96,0},{1,33},{33,65},{65,97},{97,1},{2,34}... | collective-permute-start | bytes 393224 | tf_op jit(solution)/shard_map/ppermute | solution.py:412
  70.3 2.9 %collective-permute-start.17 = (bf16[256,256]{1,0:T(8,128)(2,1)S(1)}, bf16[256,256]{1,0:T(8,128)(2,1)S(1)}, u32[]{:S(2)}, u32[]{:S(2)}) collective-permute-start(bf16[256,256]{1,0:T(8,128)(2,1)S(1)} %get-tuple-element.79), channel_id=1, source_target_pairs={{0,64},{32,96},{64,0},{96,32},{1,65},{33,97},{65,1},{97,33},{2,66}... | collective-permute-start | bytes 393224 | tf_op jit(solution)/shard_map/ppermute | solution.py:412
  73.2 1.3 %collective-permute-start.18 = (bf16[256,256]{1,0:T(8,128)(2,1)S(1)}, bf16[256,256]{1,0:T(8,128)(2,1)S(1)}, u32[]{:S(2)}, u32[]{:S(2)}) collective-permute-start(bf16[256,256]{1,0:T(8,128)(2,1)S(1)} %get-tuple-element.80), channel_id=1, source_target_pairs={{0,96},{32,0},{64,32},{96,64},{1,97},{33,1},{65,33},{97,65},{2,98}... | collective-permute-start | bytes 393224 | tf_op jit(solution)/shard_map/ppermute | solution.py:412
  74.6 1.3 %collective-permute-done.16.rest_1_ = bf16[256,256]{1,0:T(8,128)(2,1)S(1)} collective-permute-done((bf16[256,256]{1,0:T(8,128)(2,1)S(1)}, bf16[256,256]{1,0:T(8,128)(2,1)S(1)}, u32[]{:S(2)}, u32[]{:S(2)}) %collective-permute-start.16) | collective-permute-done | bytes 131104 | tf_op jit(solution)/shard_map/ppermute | solution.py:412
  75.9 4.0 %collective-permute-done.17.rest_2_ = bf16[256,256]{1,0:T(8,128)(2,1)S(1)} collective-permute-done((bf16[256,256]{1,0:T(8,128)(2,1)S(1)}, bf16[256,256]{1,0:T(8,128)(2,1)S(1)}, u32[]{:S(2)}, u32[]{:S(2)}) %collective-permute-start.17) | collective-permute-done | bytes 131104 | tf_op jit(solution)/shard_map/ppermute | solution.py:412
  79.9 0.1 add_convert_fusion
  80.0 3.3 %collective-permute-start.19 = (bf16[128,2048]{1,0:T(8,128)(2,1)S(1)}, bf16[128,2048]{1,0:T(8,128)(2,1)S(1)}, u32[]{:S(2)}, u32[]{:S(2)}) collective-permute-start(bf16[128,2048]{1,0:T(8,128)(2,1)S(1)} %add_convert_fusion), channel_id=1, source_target_pairs={{0,2},{2,0},{1,3},{3,1},{4,6},{6,4},{5,7},{7,5},{8,10},{10,8},{9,1... | collective-permute-start | bytes 1572872 | tf_op jit(solution)/shard_map/ppermute | solution.py:424
  83.3 0.6 sum_heads.1
  83.9 0.1 collective-permute-start.20
  84.0 2.1 %collective-permute-start.21 = (bf16[64,256]{1,0:T(8,128)(2,1)S(1)}, bf16[64,256]{1,0:T(8,128)(2,1)S(1)}, u32[]{:S(2)}, u32[]{:S(2)}) collective-permute-start(bf16[64,256]{1,0:T(8,128)(2,1)S(1)} %get-tuple-element.93), channel_id=1, source_target_pairs={{0,8},{4,12},{8,0},{12,4},{1,9},{5,13},{9,1},{13,5},{2,10},{6,14},... | collective-permute-start | bytes 98312 | tf_op jit(solution)/shard_map/ppermute | solution.py:412
  86.1 1.6 %collective-permute-start.22 = (bf16[64,256]{1,0:T(8,128)(2,1)S(1)}, bf16[64,256]{1,0:T(8,128)(2,1)S(1)}, u32[]{:S(2)}, u32[]{:S(2)}) collective-permute-start(bf16[64,256]{1,0:T(8,128)(2,1)S(1)} %get-tuple-element.94), channel_id=1, source_target_pairs={{0,12},{4,0},{8,4},{12,8},{1,13},{5,1},{9,5},{13,9},{2,14},{6,2},{... | collective-permute-start | bytes 98312 | tf_op jit(solution)/shard_map/ppermute | solution.py:412
  87.7 1.5 %collective-permute-done.20.rest_1_ = bf16[64,256]{1,0:T(8,128)(2,1)S(1)} collective-permute-done((bf16[64,256]{1,0:T(8,128)(2,1)S(1)}, bf16[64,256]{1,0:T(8,128)(2,1)S(1)}, u32[]{:S(2)}, u32[]{:S(2)}) %collective-permute-start.20) | collective-permute-done | bytes 32800 | tf_op jit(solution)/shard_map/ppermute | solution.py:412
  89.1 0.4 collective-permute-done.21.rest_2_
  89.5 0.8 collective-permute-done.22.rest_3_
  90.4 0.6 sum_columns.1
  90.9 1.1 %collective-permute-start.23 = (bf16[64,128]{1,0:T(8,128)(2,1)S(1)}, bf16[64,128]{1,0:T(8,128)(2,1)S(1)}, u32[]{:S(2)}, u32[]{:S(2)}) collective-permute-start(bf16[64,128]{1,0:T(8,128)(2,1)S(1)} %get-tuple-element.96), channel_id=1, source_target_pairs={{0,16},{16,0},{1,17},{17,1},{2,18},{18,2},{3,19},{19,3},{4,20},{20... | collective-permute-start | bytes 49160 | tf_op jit(solution)/shard_map/ppermute | solution.py:424
  92.0 4.1 %collective-permute-done.23 = bf16[64,128]{1,0:T(8,128)(2,1)S(1)} collective-permute-done((bf16[64,128]{1,0:T(8,128)(2,1)S(1)}, bf16[64,128]{1,0:T(8,128)(2,1)S(1)}, u32[]{:S(2)}, u32[]{:S(2)}) %collective-permute-start.23) | collective-permute-done | bytes 16416 | tf_op jit(solution)/shard_map/ppermute | solution.py:424
  96.1 0.6 convert_add_fusion.1
  96.8 1.1 %convert_add_fusion = (f32[128,1024]{1,0:T(8,128)}, bf16[128,1024]{1,0:T(8,128)(2,1)}) fusion(f32[128,2048]{1,0:T(8,128)S(1)} %get-tuple-element.75, bf16[128,2048]{1,0:T(8,128)(2,1)S(1)} %collective-permute-done.19, bf16[256,2048]{1,0:T(8,128)(2,1)S(1)} %collective-permute-done.15), kind=kLoop, calls=%fused_computation.1 | loop fusion | flops 1179648 | bytes 2883584 | tf_op jit(solution)/shard_map/add | solution.py:452
  (20 shorter events, 0.0 us)
Async XLA Ops:
  0.6 9.0 %collective-permute-start = (bf16[128,1024]{1,0:T(8,128)(2,1)}, bf16[128,1024]{1,0:T(8,128)(2,1)S(1)}, u32[]{:S(2)}, u32[]{:S(2)}) collective-permute-start(bf16[128,1024]{1,0:T(8,128)(2,1)} %own.1), channel_id=1, source_target_pairs={{0,1},{1,0},{2,3},{3,2},{4,5},{5,4},{6,7},{7,6},{8,9},{9,8},{10,11... | collective-permute-start | bytes 786440 | tf_op jit(solution)/shard_map/ppermute | solution.py:424
  0.7 8.9 %collective-permute-start.1 = (bf16[128,1024]{1,0:T(8,128)(2,1)}, bf16[128,1024]{1,0:T(8,128)(2,1)S(1)}, u32[]{:S(2)}, u32[]{:S(2)}) collective-permute-start(bf16[128,1024]{1,0:T(8,128)(2,1)} %rest_4_.1), channel_id=1, source_target_pairs={{0,1},{1,0},{2,3},{3,2},{4,5},{5,4},{6,7},{7,6},{8,9},{9,8},{10,11... | collective-permute-start | bytes 786440 | tf_op jit(solution)/shard_map/ppermute | solution.py:424
  1.2 11.4 %collective-permute-start.3 = (bf16[128,1024]{1,0:T(8,128)(2,1)}, bf16[128,1024]{1,0:T(8,128)(2,1)S(1)}, u32[]{:S(2)}, u32[]{:S(2)}) collective-permute-start(bf16[128,1024]{1,0:T(8,128)(2,1)} %own.1), channel_id=1, source_target_pairs={{0,2},{2,0},{1,3},{3,1},{4,6},{6,4},{5,7},{7,5},{8,10},{10,8},{9,1... | collective-permute-start | bytes 786440 | tf_op jit(solution)/shard_map/ppermute | solution.py:424
  5.2 12.4 %collective-permute-start.4 = (bf16[128,1024]{1,0:T(8,128)(2,1)}, bf16[128,1024]{1,0:T(8,128)(2,1)S(1)}, u32[]{:S(2)}, u32[]{:S(2)}) collective-permute-start(bf16[128,1024]{1,0:T(8,128)(2,1)} %rest_4_.1), channel_id=1, source_target_pairs={{0,2},{2,0},{1,3},{3,1},{4,6},{6,4},{5,7},{7,5},{8,10},{10,8},{9,1... | collective-permute-start | bytes 786440 | tf_op jit(solution)/shard_map/ppermute | solution.py:424
  5.3 1.6 %copy-start = (bf16[1024,1024]{1,0:T(8,128)(2,1)S(1)}, bf16[1024,1024]{1,0:T(8,128)(2,1)}, u32[]{:S(2)}) copy-start(bf16[1024,1024]{1,0:T(8,128)(2,1)} %wk.1) | copy-start | bytes 6291460
  6.9 2.8 %copy-start.1 = (bf16[128,1024]{1,0:T(8,128)(2,1)S(1)}, bf16[128,1024]{1,0:T(8,128)(2,1)}, u32[]{:S(2)}) copy-start(bf16[128,1024]{1,0:T(8,128)(2,1)} %rest_4_.1) | copy-start | bytes 786436
  6.9 2.8 %copy-start.2 = (bf16[128,1024]{1,0:T(8,128)(2,1)S(1)}, bf16[128,1024]{1,0:T(8,128)(2,1)}, u32[]{:S(2)}) copy-start(bf16[128,1024]{1,0:T(8,128)(2,1)} %own.1) | copy-start | bytes 786436
  11.1 22.5 %copy-start.3 = (s32[1,16,16]{2,1,0:T(8,128)S(1)}, s32[1,16,16]{2,1,0:T(8,128)}, u32[]{:S(2)}) copy-start(s32[1,16,16]{2,1,0:T(8,128)} %cov.1) | copy-start | bytes 3076
  11.1 6.5 %collective-permute-start.2 = (bf16[256,256]{1,0:T(8,128)(2,1)S(1)}, bf16[256,256]{1,0:T(8,128)(2,1)S(1)}, u32[]{:S(2)}, u32[]{:S(2)}) collective-permute-start(bf16[256,256]{1,0:T(8,128)(2,1)S(1)} %get-tuple-element.53), channel_id=1, source_target_pairs={{0,4},{4,8},{8,12},{12,0},{1,5},{5,9},{9,13},{13,1},{2,6},{6,10},{... | collective-permute-start | bytes 393224 | tf_op jit(solution)/shard_map/ppermute | solution.py:412
  17.6 4.7 %collective-permute-start.7 = (bf16[128,1024]{1,0:T(8,128)(2,1)S(1)}, bf16[128,1024]{1,0:T(8,128)(2,1)S(1)}, u32[]{:S(2)}, u32[]{:S(2)}) collective-permute-start(bf16[128,1024]{1,0:T(8,128)(2,1)S(1)} %collective-permute-done.3.own), channel_id=1, source_target_pairs={{0,1},{1,0},{2,3},{3,2},{4,5},{5,4},{6,7},{7,6},{8,9},{9,8},{10,11... | collective-permute-start | bytes 786440 | tf_op jit(solution)/shard_map/ppermute | solution.py:424
  17.6 4.7 %collective-permute-start.8 = (bf16[128,1024]{1,0:T(8,128)(2,1)S(1)}, bf16[128,1024]{1,0:T(8,128)(2,1)S(1)}, u32[]{:S(2)}, u32[]{:S(2)}) collective-permute-start(bf16[128,1024]{1,0:T(8,128)(2,1)S(1)} %collective-permute-done.4.cot.rest_6_), channel_id=1, source_target_pairs={{0,1},{1,0},{2,3},{3,2},{4,5},{5,4},{6,7},{7,6},{8,9},{9,8},{10,11... | collective-permute-start | bytes 786440 | tf_op jit(solution)/shard_map/ppermute | solution.py:424
  18.1 9.8 %collective-permute-start.5 = (bf16[256,256]{1,0:T(8,128)(2,1)S(1)}, bf16[256,256]{1,0:T(8,128)(2,1)S(1)}, u32[]{:S(2)}, u32[]{:S(2)}) collective-permute-start(bf16[256,256]{1,0:T(8,128)(2,1)S(1)} %get-tuple-element.55), channel_id=1, source_target_pairs={{0,8},{4,12},{8,0},{12,4},{1,9},{5,13},{9,1},{13,5},{2,10},{6,14},... | collective-permute-start | bytes 393224 | tf_op jit(solution)/shard_map/ppermute | solution.py:412
  21.1 7.1 %collective-permute-start.6 = (bf16[256,256]{1,0:T(8,128)(2,1)S(1)}, bf16[256,256]{1,0:T(8,128)(2,1)S(1)}, u32[]{:S(2)}, u32[]{:S(2)}) collective-permute-start(bf16[256,256]{1,0:T(8,128)(2,1)S(1)} %get-tuple-element.56), channel_id=1, source_target_pairs={{0,12},{4,0},{8,4},{12,8},{1,13},{5,1},{9,5},{13,9},{2,14},{6,2},{... | collective-permute-start | bytes 393224 | tf_op jit(solution)/shard_map/ppermute | solution.py:412
  23.6 8.9 %collective-permute-start.9 = (bf16[256,256]{1,0:T(8,128)(2,1)S(1)}, bf16[256,256]{1,0:T(8,128)(2,1)S(1)}, u32[]{:S(2)}, u32[]{:S(2)}) collective-permute-start(bf16[256,256]{1,0:T(8,128)(2,1)S(1)} %get-tuple-element.60), channel_id=1, source_target_pairs={{0,4},{4,8},{8,12},{12,0},{1,5},{5,9},{9,13},{13,1},{2,6},{6,10},{... | collective-permute-start | bytes 393224 | tf_op jit(solution)/shard_map/ppermute | solution.py:412
  24.6 8.0 %collective-permute-start.10 = (bf16[256,256]{1,0:T(8,128)(2,1)S(1)}, bf16[256,256]{1,0:T(8,128)(2,1)S(1)}, u32[]{:S(2)}, u32[]{:S(2)}) collective-permute-start(bf16[256,256]{1,0:T(8,128)(2,1)S(1)} %get-tuple-element.61), channel_id=1, source_target_pairs={{0,8},{4,12},{8,0},{12,4},{1,9},{5,13},{9,1},{13,5},{2,10},{6,14},... | collective-permute-start | bytes 393224 | tf_op jit(solution)/shard_map/ppermute | solution.py:412
  25.3 8.2 %collective-permute-start.11 = (bf16[256,256]{1,0:T(8,128)(2,1)S(1)}, bf16[256,256]{1,0:T(8,128)(2,1)S(1)}, u32[]{:S(2)}, u32[]{:S(2)}) collective-permute-start(bf16[256,256]{1,0:T(8,128)(2,1)S(1)} %get-tuple-element.62), channel_id=1, source_target_pairs={{0,12},{4,0},{8,4},{12,8},{1,13},{5,1},{9,5},{13,9},{2,14},{6,2},{... | collective-permute-start | bytes 393224 | tf_op jit(solution)/shard_map/ppermute | solution.py:412
  47.8 13.7 %collective-permute-start.12 = (bf16[256,512]{1,0:T(8,128)(2,1)S(1)}, bf16[256,512]{1,0:T(8,128)(2,1)S(1)}, u32[]{:S(2)}, u32[]{:S(2)}) collective-permute-start(bf16[256,512]{1,0:T(8,128)(2,1)S(1)} %get-tuple-element.64), channel_id=1, source_target_pairs={{0,12},{4,0},{8,4},{12,8},{1,13},{5,1},{9,5},{13,9},{2,14},{6,2},{... | collective-permute-start | bytes 786440 | tf_op jit(solution)/shard_map/ppermute | solution.py:412
  50.5 11.0 %collective-permute-start.13 = (bf16[256,512]{1,0:T(8,128)(2,1)S(1)}, bf16[256,512]{1,0:T(8,128)(2,1)S(1)}, u32[]{:S(2)}, u32[]{:S(2)}) collective-permute-start(bf16[256,512]{1,0:T(8,128)(2,1)S(1)} %get-tuple-element.65), channel_id=1, source_target_pairs={{0,8},{4,12},{8,0},{12,4},{1,9},{5,13},{9,1},{13,5},{2,10},{6,14},... | collective-permute-start | bytes 786440 | tf_op jit(solution)/shard_map/ppermute | solution.py:412
  51.3 13.9 %collective-permute-start.14 = (bf16[256,512]{1,0:T(8,128)(2,1)S(1)}, bf16[256,512]{1,0:T(8,128)(2,1)S(1)}, u32[]{:S(2)}, u32[]{:S(2)}) collective-permute-start(bf16[256,512]{1,0:T(8,128)(2,1)S(1)} %get-tuple-element.66), channel_id=1, source_target_pairs={{0,4},{4,8},{8,12},{12,0},{1,5},{5,9},{9,13},{13,1},{2,6},{6,10},{... | collective-permute-start | bytes 786440 | tf_op jit(solution)/shard_map/ppermute | solution.py:412
  68.6 11.3 %collective-permute-start.15 = (bf16[256,2048]{1,0:T(8,128)(2,1)S(1)}, bf16[256,2048]{1,0:T(8,128)(2,1)S(1)}, u32[]{:S(2)}, u32[]{:S(2)}) collective-permute-start(bf16[256,2048]{1,0:T(8,128)(2,1)S(1)} %get-tuple-element.76), channel_id=1, source_target_pairs={{0,1},{1,0},{2,3},{3,2},{4,5},{5,4},{6,7},{7,6},{8,9},{9,8},{10,11... | collective-permute-start | bytes 3145736 | tf_op jit(solution)/shard_map/ppermute | solution.py:424
  68.7 7.2 %collective-permute-start.16 = (bf16[256,256]{1,0:T(8,128)(2,1)S(1)}, bf16[256,256]{1,0:T(8,128)(2,1)S(1)}, u32[]{:S(2)}, u32[]{:S(2)}) collective-permute-start(bf16[256,256]{1,0:T(8,128)(2,1)S(1)} %get-tuple-element.78), channel_id=1, source_target_pairs={{0,32},{32,64},{64,96},{96,0},{1,33},{33,65},{65,97},{97,1},{2,34}... | collective-permute-start | bytes 393224 | tf_op jit(solution)/shard_map/ppermute | solution.py:412
  70.3 9.5 %collective-permute-start.17 = (bf16[256,256]{1,0:T(8,128)(2,1)S(1)}, bf16[256,256]{1,0:T(8,128)(2,1)S(1)}, u32[]{:S(2)}, u32[]{:S(2)}) collective-permute-start(bf16[256,256]{1,0:T(8,128)(2,1)S(1)} %get-tuple-element.79), channel_id=1, source_target_pairs={{0,64},{32,96},{64,0},{96,32},{1,65},{33,97},{65,1},{97,33},{2,66}... | collective-permute-start | bytes 393224 | tf_op jit(solution)/shard_map/ppermute | solution.py:412
  73.2 6.6 %collective-permute-start.18 = (bf16[256,256]{1,0:T(8,128)(2,1)S(1)}, bf16[256,256]{1,0:T(8,128)(2,1)S(1)}, u32[]{:S(2)}, u32[]{:S(2)}) collective-permute-start(bf16[256,256]{1,0:T(8,128)(2,1)S(1)} %get-tuple-element.80), channel_id=1, source_target_pairs={{0,96},{32,0},{64,32},{96,64},{1,97},{33,1},{65,33},{97,65},{2,98}... | collective-permute-start | bytes 393224 | tf_op jit(solution)/shard_map/ppermute | solution.py:412
  80.0 16.8 %collective-permute-start.19 = (bf16[128,2048]{1,0:T(8,128)(2,1)S(1)}, bf16[128,2048]{1,0:T(8,128)(2,1)S(1)}, u32[]{:S(2)}, u32[]{:S(2)}) collective-permute-start(bf16[128,2048]{1,0:T(8,128)(2,1)S(1)} %add_convert_fusion), channel_id=1, source_target_pairs={{0,2},{2,0},{1,3},{3,1},{4,6},{6,4},{5,7},{7,5},{8,10},{10,8},{9,1... | collective-permute-start | bytes 1572872 | tf_op jit(solution)/shard_map/ppermute | solution.py:424
  83.9 5.2 %collective-permute-start.20 = (bf16[64,256]{1,0:T(8,128)(2,1)S(1)}, bf16[64,256]{1,0:T(8,128)(2,1)S(1)}, u32[]{:S(2)}, u32[]{:S(2)}) collective-permute-start(bf16[64,256]{1,0:T(8,128)(2,1)S(1)} %get-tuple-element.92), channel_id=1, source_target_pairs={{0,4},{4,8},{8,12},{12,0},{1,5},{5,9},{9,13},{13,1},{2,6},{6,10},{... | collective-permute-start | bytes 98312 | tf_op jit(solution)/shard_map/ppermute | solution.py:412
  84.0 5.5 %collective-permute-start.21 = (bf16[64,256]{1,0:T(8,128)(2,1)S(1)}, bf16[64,256]{1,0:T(8,128)(2,1)S(1)}, u32[]{:S(2)}, u32[]{:S(2)}) collective-permute-start(bf16[64,256]{1,0:T(8,128)(2,1)S(1)} %get-tuple-element.93), channel_id=1, source_target_pairs={{0,8},{4,12},{8,0},{12,4},{1,9},{5,13},{9,1},{13,5},{2,10},{6,14},... | collective-permute-start | bytes 98312 | tf_op jit(solution)/shard_map/ppermute | solution.py:412
  86.1 4.3 %collective-permute-start.22 = (bf16[64,256]{1,0:T(8,128)(2,1)S(1)}, bf16[64,256]{1,0:T(8,128)(2,1)S(1)}, u32[]{:S(2)}, u32[]{:S(2)}) collective-permute-start(bf16[64,256]{1,0:T(8,128)(2,1)S(1)} %get-tuple-element.94), channel_id=1, source_target_pairs={{0,12},{4,0},{8,4},{12,8},{1,13},{5,1},{9,5},{13,9},{2,14},{6,2},{... | collective-permute-start | bytes 98312 | tf_op jit(solution)/shard_map/ppermute | solution.py:412
  90.9 5.2 %collective-permute-start.23 = (bf16[64,128]{1,0:T(8,128)(2,1)S(1)}, bf16[64,128]{1,0:T(8,128)(2,1)S(1)}, u32[]{:S(2)}, u32[]{:S(2)}) collective-permute-start(bf16[64,128]{1,0:T(8,128)(2,1)S(1)} %get-tuple-element.96), channel_id=1, source_target_pairs={{0,16},{16,0},{1,17},{17,1},{2,18},{18,2},{3,19},{19,3},{4,20},{20... | collective-permute-start | bytes 49160 | tf_op jit(solution)/shard_map/ppermute | solution.py:424

commit v2 on v1

--- a/solution.py
+++ b/solution.py
@@ -440,7 +440,7 @@
     terms, cuts = lax.optimization_barrier((terms, cuts))
     cuts = shifted(cuts, "sy", 1)
     own, far_own, away = finish(place, terms, weights)
-    sent, cuts = lax.optimization_barrier((across(away, "fc"), cuts))
+    sent, cuts[2] = lax.optimization_barrier((across(away, "fc"), cuts[2]))
     rows, width = tokens.shape
     far_sum = (far_own + sent[rows:].astype(F32)).astype(BF)
     cuts, _ = lax.optimization_barrier((cuts, far_sum))

time: 98 us -> 99.5 us (1.015)
    ppermute x15, waiting for transfers between devices: 27.4 us -> 29.6 us  [shifted(): lax.ppermute(parts[d], axis, [(i, (i + sign * d) % size) for i in range(s...]
    ppermute x9, waiting for transfers between devices: 9.07 us -> 7.68 us  [across(): return lax.ppermute(part, axis, swap)]
  transfers between devices with their start and end apart: 24 -> 24, of which waited for: 12 -> 13; matrix products, arithmetic and copies ran while one was open for 1% -> 1% of each run, Pallas kernels for 7% -> 7%
where the time goes in v2:
time: 99.5 us; the launch traced here: 99.3 us
  waiting for transfers between devices  37.3 us (37%)
  starting transfers between devices  33.4 us (34%)
  Pallas kernels  24.3 us (24%)
  other arithmetic  1.84 us (2%)
  local copies, waits for them, and re-layouts  1.69 us (2%)
    ppermute x15, waiting for transfers between devices, shifted(): lax.ppermute(parts[d], axis, [(i, (i + sign * d) % size) for i in range(s...  29.6 us
    ppermute x15, starting transfers between devices, shifted(): lax.ppermute(parts[d], axis, [(i, (i + sign * d) % size) for i in range(s...  23.8 us
    pallas_call x1, Pallas kernels, attend(): pl.pallas_call(functools.partial(attend_kernel, chips, step, 1024), in_sp...  14.3 us
    ppermute x9, starting transfers between devices, across(): return lax.ppermute(part, axis, swap)  9.6 us
    ppermute x9, waiting for transfers between devices, across(): return lax.ppermute(part, axis, swap)  7.68 us
    pallas_call x2, Pallas kernels, project(): pl.pallas_call(project_kernel, in_specs=[SMEM] + [VMEM] * 6, out_specs=[V...  2.74 us
    pallas_call x1, Pallas kernels, fetch(): pl.pallas_call(fetch_kernel, in_specs=[SMEM] + [ANY] * 4, out_specs=[VMEM...  2.73 us
    pallas_call x1, Pallas kernels, finish(): pl.pallas_call(finish_kernel, in_specs=[SMEM] + [VMEM] * (2 + chips), out...  2.13 us
  transfers between devices with their start and end apart: 24, of which 13 were waited for; matrix products, arithmetic and copies ran while one was open for 1% of the time, Pallas kernels for 7%

profile of v2, /device:TPU:0, one launch (start us, length us, event | category | flops | bytes accessed | tf_op | source)
XLA Modules:
  0.0 99.3 jit_solution(11819910278805624710)
XLA Ops:
  0.6 0.1 collective-permute-start
  0.7 0.5 collective-permute-start.1
  1.2 4.0 %collective-permute-start.3 = (bf16[128,1024]{1,0:T(8,128)(2,1)}, bf16[128,1024]{1,0:T(8,128)(2,1)S(1)}, u32[]{:S(2)}, u32[]{:S(2)}) collective-permute-start(bf16[128,1024]{1,0:T(8,128)(2,1)} %own.1), channel_id=1, source_target_pairs={{0,2},{2,0},{1,3},{3,1},{4,6},{6,4},{5,7},{7,5},{8,10},{10,8},{9,1... | collective-permute-start | bytes 786440 | tf_op jit(solution)/shard_map/ppermute | solution.py:424
  5.2 0.1 stack.27.place
  5.3 1.6 %copy-done = bf16[1024,1024]{1,0:T(8,128)(2,1)S(1)} copy-done((bf16[1024,1024]{1,0:T(8,128)(2,1)S(1)}, bf16[1024,1024]{1,0:T(8,128)(2,1)}, u32[]{:S(2)}) %copy-start) | copy-done | bytes 2097176
  6.9 2.7 %fetch.1 = (bf16[3,1024,256]{2,1,0:T(8,128)(2,1)S(1)}, bf16[256,1024]{1,0:T(8,128)(2,1)S(1)}) custom-call(s32[6]{0:T(128)S(1)} %stack.27.place, bf16[1024,1024]{1,0:T(8,128)(2,1)S(1)} %copy-done, bf16[1024,1024]{1,0:T(8,128)(2,1)} %wv.1, bf16[1024,1024]{1,0:T(8,128)(2,1)} %wq.1, bf16[1024,1024]{1,0:T(8,128)(2,1)} %wo.1), custom_call_target="tpu_custom_call" | custom-call | flops 1 | bytes 1 | tf_op jit(solution)/shard_map/fetch/pallas_call | solution.py:87
  9.7 1.4 %project.2 = (bf16[256,256]{1,0:T(8,128)(2,1)S(1)}, bf16[256,256]{1,0:T(8,128)(2,1)S(1)}, bf16[256,256]{1,0:T(8,128)(2,1)S(1)}, bf16[256,256]{1,0:T(8,128)(2,1)S(1)}) custom-call(s32[6]{0:T(128)S(1)} %stack.27.place, bf16[128,1024]{1,0:T(8,128)(2,1)S(1)} %copy-done.2, bf16[128,1024]{1,0:T(8,128)(2,1)S(1)} %collective-permute-done.peer, ...), custom_call_target="tpu_custom_call" | custom-call | flops 1 | bytes 1 | tf_op jit(solution)/shard_map/project/pallas_call | solution.py:120
  11.1 1.6 %collective-permute-start.2 = (bf16[256,256]{1,0:T(8,128)(2,1)S(1)}, bf16[256,256]{1,0:T(8,128)(2,1)S(1)}, u32[]{:S(2)}, u32[]{:S(2)}) collective-permute-start(bf16[256,256]{1,0:T(8,128)(2,1)S(1)} %get-tuple-element.50), channel_id=1, source_target_pairs={{0,4},{4,8},{8,12},{12,0},{1,5},{5,9},{9,13},{13,1},{2,6},{6,10},{... | collective-permute-start | bytes 393224 | tf_op jit(solution)/shard_map/ppermute | solution.py:412
  12.6 4.9 %collective-permute-done.4.cot.rest_6_ = bf16[128,1024]{1,0:T(8,128)(2,1)S(1)} collective-permute-done((bf16[128,1024]{1,0:T(8,128)(2,1)}, bf16[128,1024]{1,0:T(8,128)(2,1)S(1)}, u32[]{:S(2)}, u32[]{:S(2)}) %collective-permute-start.4) | collective-permute-done | bytes 262176 | tf_op jit(solution)/shard_map/ppermute | solution.py:424
  17.6 0.5 collective-permute-start.8
  18.1 3.0 %collective-permute-start.5 = (bf16[256,256]{1,0:T(8,128)(2,1)S(1)}, bf16[256,256]{1,0:T(8,128)(2,1)S(1)}, u32[]{:S(2)}, u32[]{:S(2)}) collective-permute-start(bf16[256,256]{1,0:T(8,128)(2,1)S(1)} %get-tuple-element.52), channel_id=1, source_target_pairs={{0,8},{4,12},{8,0},{12,4},{1,9},{5,13},{9,1},{13,5},{2,10},{6,14},... | collective-permute-start | bytes 393224 | tf_op jit(solution)/shard_map/ppermute | solution.py:412
  21.1 1.1 %collective-permute-start.6 = (bf16[256,256]{1,0:T(8,128)(2,1)S(1)}, bf16[256,256]{1,0:T(8,128)(2,1)S(1)}, u32[]{:S(2)}, u32[]{:S(2)}) collective-permute-start(bf16[256,256]{1,0:T(8,128)(2,1)S(1)} %get-tuple-element.53), channel_id=1, source_target_pairs={{0,12},{4,0},{8,4},{12,8},{1,13},{5,1},{9,5},{13,9},{2,14},{6,2},{... | collective-permute-start | bytes 393224 | tf_op jit(solution)/shard_map/ppermute | solution.py:412
  22.3 1.4 %project.3 = (bf16[256,256]{1,0:T(8,128)(2,1)S(1)}, bf16[256,256]{1,0:T(8,128)(2,1)S(1)}, bf16[256,256]{1,0:T(8,128)(2,1)S(1)}, bf16[256,256]{1,0:T(8,128)(2,1)S(1)}) custom-call(s32[6]{0:T(128)S(1)} %stack.27.place, bf16[128,1024]{1,0:T(8,128)(2,1)S(1)} %collective-permute-done.3.own, bf16[128,1024]{1,0:T(8,128)(2,1)S(1)} %collective-permute-done.7.peer, ...), custom_call_target="tpu_custom_call" | custom-call | flops 1 | bytes 1 | tf_op jit(solution)/shard_map/project/pallas_call | solution.py:120
  23.6 1.0 collective-permute-start.9
  24.6 0.7 collective-permute-start.10
  25.3 2.5 %collective-permute-start.11 = (bf16[256,256]{1,0:T(8,128)(2,1)S(1)}, bf16[256,256]{1,0:T(8,128)(2,1)S(1)}, u32[]{:S(2)}, u32[]{:S(2)}) collective-permute-start(bf16[256,256]{1,0:T(8,128)(2,1)S(1)} %get-tuple-element.59), channel_id=1, source_target_pairs={{0,12},{4,0},{8,4},{12,8},{1,13},{5,1},{9,5},{13,9},{2,14},{6,2},{... | collective-permute-start | bytes 393224 | tf_op jit(solution)/shard_map/ppermute | solution.py:412
  27.9 0.3 collective-permute-done.6.rest_3_
  28.2 4.4 %collective-permute-done.9.rest_5_ = bf16[256,256]{1,0:T(8,128)(2,1)S(1)} collective-permute-done((bf16[256,256]{1,0:T(8,128)(2,1)S(1)}, bf16[256,256]{1,0:T(8,128)(2,1)S(1)}, u32[]{:S(2)}, u32[]{:S(2)}) %collective-permute-start.9) | collective-permute-done | bytes 131104 | tf_op jit(solution)/shard_map/ppermute | solution.py:412
  32.6 1.0 collective-permute-done.11.rest_7_
  33.6 14.3 %attend.1 = (bf16[256,512]{1,0:T(8,128)(2,1)S(1)}, bf16[256,512]{1,0:T(8,128)(2,1)S(1)}, bf16[256,512]{1,0:T(8,128)(2,1)S(1)}, bf16[256,512]{1,0:T(8,128)(2,1)S(1)}) custom-call(s32[6]{0:T(128)S(1)} %stack.27.place, s32[1,16,16]{2,1,0:T(8,128)S(1)} %copy-done.3, bf16[256,256]{1,0:T(8,128)(2,1)S(1)} %get-tuple-element.49.rest_0_, ...), custom_call_target="tpu_custom_call" | custom-call | flops 1 | bytes 1 | tf_op jit(solution)/shard_map/attend/pallas_call | solution.py:270
  47.8 2.7 %collective-permute-start.12 = (bf16[256,512]{1,0:T(8,128)(2,1)S(1)}, bf16[256,512]{1,0:T(8,128)(2,1)S(1)}, u32[]{:S(2)}, u32[]{:S(2)}) collective-permute-start(bf16[256,512]{1,0:T(8,128)(2,1)S(1)} %get-tuple-element.61), channel_id=1, source_target_pairs={{0,12},{4,0},{8,4},{12,8},{1,13},{5,1},{9,5},{13,9},{2,14},{6,2},{... | collective-permute-start | bytes 786440 | tf_op jit(solution)/shard_map/ppermute | solution.py:412
  50.5 0.8 collective-permute-start.13
  51.3 0.2 collective-permute-start.14
  51.5 10.1 %collective-permute-done.12.rest_1_ = bf16[256,512]{1,0:T(8,128)(2,1)S(1)} collective-permute-done((bf16[256,512]{1,0:T(8,128)(2,1)S(1)}, bf16[256,512]{1,0:T(8,128)(2,1)S(1)}, u32[]{:S(2)}, u32[]{:S(2)}) %collective-permute-start.12) | collective-permute-done | bytes 262176 | tf_op jit(solution)/shard_map/ppermute | solution.py:412
  61.6 3.7 %collective-permute-done.14.rest_3_ = bf16[256,512]{1,0:T(8,128)(2,1)S(1)} collective-permute-done((bf16[256,512]{1,0:T(8,128)(2,1)S(1)}, bf16[256,512]{1,0:T(8,128)(2,1)S(1)}, u32[]{:S(2)}, u32[]{:S(2)}) %collective-permute-start.14) | collective-permute-done | bytes 262176 | tf_op jit(solution)/shard_map/ppermute | solution.py:412
  65.3 1.2 %out_terms.1 = (bf16[256,256]{1,0:T(8,128)(2,1)S(1)}, bf16[256,256]{1,0:T(8,128)(2,1)S(1)}, bf16[256,256]{1,0:T(8,128)(2,1)S(1)}, bf16[256,256]{1,0:T(8,128)(2,1)S(1)}) custom-call(s32[6]{0:T(128)S(1)} %stack.27.place, bf16[256,512]{1,0:T(8,128)(2,1)S(1)} %get-tuple-element.68.rest_0_, bf16[256,512]{1,0:T(8,128)(2,1)S(1)} %collective-permute-done.12.rest_1_, ...), custom_call_target="tpu_custom_call" | custom-call | flops 1 | bytes 1 | tf_op jit(solution)/shard_map/out_terms/pallas_call | solution.py:345
  66.5 2.1 %finish.1 = (f32[128,2048]{1,0:T(8,128)S(1)}, f32[128,2048]{1,0:T(8,128)S(1)}, bf16[256,2048]{1,0:T(8,128)(2,1)S(1)}) custom-call(s32[6]{0:T(128)S(1)} %stack.27.place, bf16[3,1024,256]{2,1,0:T(8,128)(2,1)S(1)} %get-tuple-element.47.held, bf16[256,1024]{1,0:T(8,128)(2,1)S(1)} %get-tuple-element.48.held_out, bf16[256,512]{1,0:T(8,128)(2,1)S(1)} %get-tuple-element.68.rest_0_, ...), custom_call_target="tpu_custom_call" | custom-call | flops 1 | bytes 1 | tf_op jit(solution)/shard_map/finish/pallas_call | solution.py:317
  68.6 0.1 collective-permute-start.15
  68.7 3.3 %collective-permute-start.16 = (bf16[256,256]{1,0:T(8,128)(2,1)S(1)}, bf16[256,256]{1,0:T(8,128)(2,1)S(1)}, u32[]{:S(2)}, u32[]{:S(2)}) collective-permute-start(bf16[256,256]{1,0:T(8,128)(2,1)S(1)} %get-tuple-element.74), channel_id=1, source_target_pairs={{0,64},{32,96},{64,0},{96,32},{1,65},{33,97},{65,1},{97,33},{2,66}... | collective-permute-start | bytes 393224 | tf_op jit(solution)/shard_map/ppermute | solution.py:412
  72.0 4.1 %collective-permute-done.16.rest_2_ = bf16[256,256]{1,0:T(8,128)(2,1)S(1)} collective-permute-done((bf16[256,256]{1,0:T(8,128)(2,1)S(1)}, bf16[256,256]{1,0:T(8,128)(2,1)S(1)}, u32[]{:S(2)}, u32[]{:S(2)}) %collective-permute-start.16) | collective-permute-done | bytes 131104 | tf_op jit(solution)/shard_map/ppermute | solution.py:412
  76.1 0.1 add_convert_fusion
  76.2 3.3 %collective-permute-start.17 = (bf16[128,2048]{1,0:T(8,128)(2,1)S(1)}, bf16[128,2048]{1,0:T(8,128)(2,1)S(1)}, u32[]{:S(2)}, u32[]{:S(2)}) collective-permute-start(bf16[128,2048]{1,0:T(8,128)(2,1)S(1)} %add_convert_fusion), channel_id=1, source_target_pairs={{0,2},{2,0},{1,3},{3,1},{4,6},{6,4},{5,7},{7,5},{8,10},{10,8},{9,1... | collective-permute-start | bytes 1572872 | tf_op jit(solution)/shard_map/ppermute | solution.py:424
  79.5 1.6 %collective-permute-start.18 = (bf16[256,256]{1,0:T(8,128)(2,1)S(1)}, bf16[256,256]{1,0:T(8,128)(2,1)S(1)}, u32[]{:S(2)}, u32[]{:S(2)}) collective-permute-start(bf16[256,256]{1,0:T(8,128)(2,1)S(1)} %get-tuple-element.78), channel_id=1, source_target_pairs={{0,32},{32,64},{64,96},{96,0},{1,33},{33,65},{65,97},{97,1},{2,34}... | collective-permute-start | bytes 393224 | tf_op jit(solution)/shard_map/ppermute | solution.py:412
  81.1 1.7 %collective-permute-start.19 = (bf16[256,256]{1,0:T(8,128)(2,1)S(1)}, bf16[256,256]{1,0:T(8,128)(2,1)S(1)}, u32[]{:S(2)}, u32[]{:S(2)}) collective-permute-start(bf16[256,256]{1,0:T(8,128)(2,1)S(1)} %get-tuple-element.80), channel_id=1, source_target_pairs={{0,96},{32,0},{64,32},{96,64},{1,97},{33,1},{65,33},{97,65},{2,98}... | collective-permute-start | bytes 393224 | tf_op jit(solution)/shard_map/ppermute | solution.py:412
  82.8 2.9 %collective-permute-done.18.rest_1_ = bf16[256,256]{1,0:T(8,128)(2,1)S(1)} collective-permute-done((bf16[256,256]{1,0:T(8,128)(2,1)S(1)}, bf16[256,256]{1,0:T(8,128)(2,1)S(1)}, u32[]{:S(2)}, u32[]{:S(2)}) %collective-permute-start.18) | collective-permute-done | bytes 131104 | tf_op jit(solution)/shard_map/ppermute | solution.py:412
  85.7 0.4 collective-permute-done.19.rest_3_
  86.1 0.6 sum_heads.1
  86.7 0.1 collective-permute-start.20
  86.8 2.1 %collective-permute-start.21 = (bf16[64,256]{1,0:T(8,128)(2,1)S(1)}, bf16[64,256]{1,0:T(8,128)(2,1)S(1)}, u32[]{:S(2)}, u32[]{:S(2)}) collective-permute-start(bf16[64,256]{1,0:T(8,128)(2,1)S(1)} %get-tuple-element.87), channel_id=1, source_target_pairs={{0,8},{4,12},{8,0},{12,4},{1,9},{5,13},{9,1},{13,5},{2,10},{6,14},... | collective-permute-start | bytes 98312 | tf_op jit(solution)/shard_map/ppermute | solution.py:412
  88.9 1.6 %collective-permute-start.22 = (bf16[64,256]{1,0:T(8,128)(2,1)S(1)}, bf16[64,256]{1,0:T(8,128)(2,1)S(1)}, u32[]{:S(2)}, u32[]{:S(2)}) collective-permute-start(bf16[64,256]{1,0:T(8,128)(2,1)S(1)} %get-tuple-element.88), channel_id=1, source_target_pairs={{0,12},{4,0},{8,4},{12,8},{1,13},{5,1},{9,5},{13,9},{2,14},{6,2},{... | collective-permute-start | bytes 98312 | tf_op jit(solution)/shard_map/ppermute | solution.py:412
  90.5 1.5 %collective-permute-done.20.rest_1_ = bf16[64,256]{1,0:T(8,128)(2,1)S(1)} collective-permute-done((bf16[64,256]{1,0:T(8,128)(2,1)S(1)}, bf16[64,256]{1,0:T(8,128)(2,1)S(1)}, u32[]{:S(2)}, u32[]{:S(2)}) %collective-permute-start.20) | collective-permute-done | bytes 32800 | tf_op jit(solution)/shard_map/ppermute | solution.py:412
  91.9 0.4 collective-permute-done.21.rest_2_
  92.3 0.8 collective-permute-done.22.rest_3_
  93.1 0.6 sum_columns.1
  93.7 1.1 %collective-permute-start.23 = (bf16[64,128]{1,0:T(8,128)(2,1)S(1)}, bf16[64,128]{1,0:T(8,128)(2,1)S(1)}, u32[]{:S(2)}, u32[]{:S(2)}) collective-permute-start(bf16[64,128]{1,0:T(8,128)(2,1)S(1)} %get-tuple-element.90), channel_id=1, source_target_pairs={{0,16},{16,0},{1,17},{17,1},{2,18},{18,2},{3,19},{19,3},{4,20},{20... | collective-permute-start | bytes 49160 | tf_op jit(solution)/shard_map/ppermute | solution.py:424
  94.8 2.7 %collective-permute-done.23 = bf16[64,128]{1,0:T(8,128)(2,1)S(1)} collective-permute-done((bf16[64,128]{1,0:T(8,128)(2,1)S(1)}, bf16[64,128]{1,0:T(8,128)(2,1)S(1)}, u32[]{:S(2)}, u32[]{:S(2)}) %collective-permute-start.23) | collective-permute-done | bytes 16416 | tf_op jit(solution)/shard_map/ppermute | solution.py:424
  97.5 0.6 convert_add_fusion.1
  98.2 1.1 %convert_add_fusion = (f32[128,1024]{1,0:T(8,128)}, bf16[128,1024]{1,0:T(8,128)(2,1)}) fusion(f32[128,2048]{1,0:T(8,128)S(1)} %get-tuple-element.72, bf16[128,2048]{1,0:T(8,128)(2,1)S(1)} %collective-permute-done.17, bf16[256,2048]{1,0:T(8,128)(2,1)S(1)} %collective-permute-done.15), kind=kLoop, calls=%fused_computation.1 | loop fusion | flops 1179648 | bytes 2883584 | tf_op jit(solution)/shard_map/add | solution.py:452
  (20 shorter events, 0.1 us)
Async XLA Ops:
  0.6 9.0 %collective-permute-start = (bf16[128,1024]{1,0:T(8,128)(2,1)}, bf16[128,1024]{1,0:T(8,128)(2,1)S(1)}, u32[]{:S(2)}, u32[]{:S(2)}) collective-permute-start(bf16[128,1024]{1,0:T(8,128)(2,1)} %own.1), channel_id=1, source_target_pairs={{0,1},{1,0},{2,3},{3,2},{4,5},{5,4},{6,7},{7,6},{8,9},{9,8},{10,11... | collective-permute-start | bytes 786440 | tf_op jit(solution)/shard_map/ppermute | solution.py:424
  0.7 8.9 %collective-permute-start.1 = (bf16[128,1024]{1,0:T(8,128)(2,1)}, bf16[128,1024]{1,0:T(8,128)(2,1)S(1)}, u32[]{:S(2)}, u32[]{:S(2)}) collective-permute-start(bf16[128,1024]{1,0:T(8,128)(2,1)} %rest_4_.1), channel_id=1, source_target_pairs={{0,1},{1,0},{2,3},{3,2},{4,5},{5,4},{6,7},{7,6},{8,9},{9,8},{10,11... | collective-permute-start | bytes 786440 | tf_op jit(solution)/shard_map/ppermute | solution.py:424
  1.2 11.4 %collective-permute-start.3 = (bf16[128,1024]{1,0:T(8,128)(2,1)}, bf16[128,1024]{1,0:T(8,128)(2,1)S(1)}, u32[]{:S(2)}, u32[]{:S(2)}) collective-permute-start(bf16[128,1024]{1,0:T(8,128)(2,1)} %own.1), channel_id=1, source_target_pairs={{0,2},{2,0},{1,3},{3,1},{4,6},{6,4},{5,7},{7,5},{8,10},{10,8},{9,1... | collective-permute-start | bytes 786440 | tf_op jit(solution)/shard_map/ppermute | solution.py:424
  5.2 12.4 %collective-permute-start.4 = (bf16[128,1024]{1,0:T(8,128)(2,1)}, bf16[128,1024]{1,0:T(8,128)(2,1)S(1)}, u32[]{:S(2)}, u32[]{:S(2)}) collective-permute-start(bf16[128,1024]{1,0:T(8,128)(2,1)} %rest_4_.1), channel_id=1, source_target_pairs={{0,2},{2,0},{1,3},{3,1},{4,6},{6,4},{5,7},{7,5},{8,10},{10,8},{9,1... | collective-permute-start | bytes 786440 | tf_op jit(solution)/shard_map/ppermute | solution.py:424
  5.3 1.6 %copy-start = (bf16[1024,1024]{1,0:T(8,128)(2,1)S(1)}, bf16[1024,1024]{1,0:T(8,128)(2,1)}, u32[]{:S(2)}) copy-start(bf16[1024,1024]{1,0:T(8,128)(2,1)} %wk.1) | copy-start | bytes 6291460
  6.9 2.8 %copy-start.1 = (bf16[128,1024]{1,0:T(8,128)(2,1)S(1)}, bf16[128,1024]{1,0:T(8,128)(2,1)}, u32[]{:S(2)}) copy-start(bf16[128,1024]{1,0:T(8,128)(2,1)} %rest_4_.1) | copy-start | bytes 786436
  6.9 2.8 %copy-start.2 = (bf16[128,1024]{1,0:T(8,128)(2,1)S(1)}, bf16[128,1024]{1,0:T(8,128)(2,1)}, u32[]{:S(2)}) copy-start(bf16[128,1024]{1,0:T(8,128)(2,1)} %own.1) | copy-start | bytes 786436
  11.1 22.5 %copy-start.3 = (s32[1,16,16]{2,1,0:T(8,128)S(1)}, s32[1,16,16]{2,1,0:T(8,128)}, u32[]{:S(2)}) copy-start(s32[1,16,16]{2,1,0:T(8,128)} %cov.1) | copy-start | bytes 3076
  11.1 6.5 %collective-permute-start.2 = (bf16[256,256]{1,0:T(8,128)(2,1)S(1)}, bf16[256,256]{1,0:T(8,128)(2,1)S(1)}, u32[]{:S(2)}, u32[]{:S(2)}) collective-permute-start(bf16[256,256]{1,0:T(8,128)(2,1)S(1)} %get-tuple-element.50), channel_id=1, source_target_pairs={{0,4},{4,8},{8,12},{12,0},{1,5},{5,9},{9,13},{13,1},{2,6},{6,10},{... | collective-permute-start | bytes 393224 | tf_op jit(solution)/shard_map/ppermute | solution.py:412
  17.6 4.7 %collective-permute-start.7 = (bf16[128,1024]{1,0:T(8,128)(2,1)S(1)}, bf16[128,1024]{1,0:T(8,128)(2,1)S(1)}, u32[]{:S(2)}, u32[]{:S(2)}) collective-permute-start(bf16[128,1024]{1,0:T(8,128)(2,1)S(1)} %collective-permute-done.3.own), channel_id=1, source_target_pairs={{0,1},{1,0},{2,3},{3,2},{4,5},{5,4},{6,7},{7,6},{8,9},{9,8},{10,11... | collective-permute-start | bytes 786440 | tf_op jit(solution)/shard_map/ppermute | solution.py:424
  17.6 4.7 %collective-permute-start.8 = (bf16[128,1024]{1,0:T(8,128)(2,1)S(1)}, bf16[128,1024]{1,0:T(8,128)(2,1)S(1)}, u32[]{:S(2)}, u32[]{:S(2)}) collective-permute-start(bf16[128,1024]{1,0:T(8,128)(2,1)S(1)} %collective-permute-done.4.cot.rest_6_), channel_id=1, source_target_pairs={{0,1},{1,0},{2,3},{3,2},{4,5},{5,4},{6,7},{7,6},{8,9},{9,8},{10,11... | collective-permute-start | bytes 786440 | tf_op jit(solution)/shard_map/ppermute | solution.py:424
  18.1 9.8 %collective-permute-start.5 = (bf16[256,256]{1,0:T(8,128)(2,1)S(1)}, bf16[256,256]{1,0:T(8,128)(2,1)S(1)}, u32[]{:S(2)}, u32[]{:S(2)}) collective-permute-start(bf16[256,256]{1,0:T(8,128)(2,1)S(1)} %get-tuple-element.52), channel_id=1, source_target_pairs={{0,8},{4,12},{8,0},{12,4},{1,9},{5,13},{9,1},{13,5},{2,10},{6,14},... | collective-permute-start | bytes 393224 | tf_op jit(solution)/shard_map/ppermute | solution.py:412
  21.1 7.1 %collective-permute-start.6 = (bf16[256,256]{1,0:T(8,128)(2,1)S(1)}, bf16[256,256]{1,0:T(8,128)(2,1)S(1)}, u32[]{:S(2)}, u32[]{:S(2)}) collective-permute-start(bf16[256,256]{1,0:T(8,128)(2,1)S(1)} %get-tuple-element.53), channel_id=1, source_target_pairs={{0,12},{4,0},{8,4},{12,8},{1,13},{5,1},{9,5},{13,9},{2,14},{6,2},{... | collective-permute-start | bytes 393224 | tf_op jit(solution)/shard_map/ppermute | solution.py:412
  23.6 8.9 %collective-permute-start.9 = (bf16[256,256]{1,0:T(8,128)(2,1)S(1)}, bf16[256,256]{1,0:T(8,128)(2,1)S(1)}, u32[]{:S(2)}, u32[]{:S(2)}) collective-permute-start(bf16[256,256]{1,0:T(8,128)(2,1)S(1)} %get-tuple-element.57), channel_id=1, source_target_pairs={{0,4},{4,8},{8,12},{12,0},{1,5},{5,9},{9,13},{13,1},{2,6},{6,10},{... | collective-permute-start | bytes 393224 | tf_op jit(solution)/shard_map/ppermute | solution.py:412
  24.6 8.0 %collective-permute-start.10 = (bf16[256,256]{1,0:T(8,128)(2,1)S(1)}, bf16[256,256]{1,0:T(8,128)(2,1)S(1)}, u32[]{:S(2)}, u32[]{:S(2)}) collective-permute-start(bf16[256,256]{1,0:T(8,128)(2,1)S(1)} %get-tuple-element.58), channel_id=1, source_target_pairs={{0,8},{4,12},{8,0},{12,4},{1,9},{5,13},{9,1},{13,5},{2,10},{6,14},... | collective-permute-start | bytes 393224 | tf_op jit(solution)/shard_map/ppermute | solution.py:412
  25.3 8.2 %collective-permute-start.11 = (bf16[256,256]{1,0:T(8,128)(2,1)S(1)}, bf16[256,256]{1,0:T(8,128)(2,1)S(1)}, u32[]{:S(2)}, u32[]{:S(2)}) collective-permute-start(bf16[256,256]{1,0:T(8,128)(2,1)S(1)} %get-tuple-element.59), channel_id=1, source_target_pairs={{0,12},{4,0},{8,4},{12,8},{1,13},{5,1},{9,5},{13,9},{2,14},{6,2},{... | collective-permute-start | bytes 393224 | tf_op jit(solution)/shard_map/ppermute | solution.py:412
  47.8 13.7 %collective-permute-start.12 = (bf16[256,512]{1,0:T(8,128)(2,1)S(1)}, bf16[256,512]{1,0:T(8,128)(2,1)S(1)}, u32[]{:S(2)}, u32[]{:S(2)}) collective-permute-start(bf16[256,512]{1,0:T(8,128)(2,1)S(1)} %get-tuple-element.61), channel_id=1, source_target_pairs={{0,12},{4,0},{8,4},{12,8},{1,13},{5,1},{9,5},{13,9},{2,14},{6,2},{... | collective-permute-start | bytes 786440 | tf_op jit(solution)/shard_map/ppermute | solution.py:412
  50.5 11.0 %collective-permute-start.13 = (bf16[256,512]{1,0:T(8,128)(2,1)S(1)}, bf16[256,512]{1,0:T(8,128)(2,1)S(1)}, u32[]{:S(2)}, u32[]{:S(2)}) collective-permute-start(bf16[256,512]{1,0:T(8,128)(2,1)S(1)} %get-tuple-element.62), channel_id=1, source_target_pairs={{0,8},{4,12},{8,0},{12,4},{1,9},{5,13},{9,1},{13,5},{2,10},{6,14},... | collective-permute-start | bytes 786440 | tf_op jit(solution)/shard_map/ppermute | solution.py:412
  51.3 13.9 %collective-permute-start.14 = (bf16[256,512]{1,0:T(8,128)(2,1)S(1)}, bf16[256,512]{1,0:T(8,128)(2,1)S(1)}, u32[]{:S(2)}, u32[]{:S(2)}) collective-permute-start(bf16[256,512]{1,0:T(8,128)(2,1)S(1)} %get-tuple-element.63), channel_id=1, source_target_pairs={{0,4},{4,8},{8,12},{12,0},{1,5},{5,9},{9,13},{13,1},{2,6},{6,10},{... | collective-permute-start | bytes 786440 | tf_op jit(solution)/shard_map/ppermute | solution.py:412
  68.6 7.5 %collective-permute-start.15 = (bf16[256,2048]{1,0:T(8,128)(2,1)S(1)}, bf16[256,2048]{1,0:T(8,128)(2,1)S(1)}, u32[]{:S(2)}, u32[]{:S(2)}) collective-permute-start(bf16[256,2048]{1,0:T(8,128)(2,1)S(1)} %get-tuple-element.73), channel_id=1, source_target_pairs={{0,1},{1,0},{2,3},{3,2},{4,5},{5,4},{6,7},{7,6},{8,9},{9,8},{10,11... | collective-permute-start | bytes 3145736 | tf_op jit(solution)/shard_map/ppermute | solution.py:424
  68.7 7.4 %collective-permute-start.16 = (bf16[256,256]{1,0:T(8,128)(2,1)S(1)}, bf16[256,256]{1,0:T(8,128)(2,1)S(1)}, u32[]{:S(2)}, u32[]{:S(2)}) collective-permute-start(bf16[256,256]{1,0:T(8,128)(2,1)S(1)} %get-tuple-element.74), channel_id=1, source_target_pairs={{0,64},{32,96},{64,0},{96,32},{1,65},{33,97},{65,1},{97,33},{2,66}... | collective-permute-start | bytes 393224 | tf_op jit(solution)/shard_map/ppermute | solution.py:412
  76.2 21.9 %collective-permute-start.17 = (bf16[128,2048]{1,0:T(8,128)(2,1)S(1)}, bf16[128,2048]{1,0:T(8,128)(2,1)S(1)}, u32[]{:S(2)}, u32[]{:S(2)}) collective-permute-start(bf16[128,2048]{1,0:T(8,128)(2,1)S(1)} %add_convert_fusion), channel_id=1, source_target_pairs={{0,2},{2,0},{1,3},{3,1},{4,6},{6,4},{5,7},{7,5},{8,10},{10,8},{9,1... | collective-permute-start | bytes 1572872 | tf_op jit(solution)/shard_map/ppermute | solution.py:424
  79.5 6.2 %collective-permute-start.18 = (bf16[256,256]{1,0:T(8,128)(2,1)S(1)}, bf16[256,256]{1,0:T(8,128)(2,1)S(1)}, u32[]{:S(2)}, u32[]{:S(2)}) collective-permute-start(bf16[256,256]{1,0:T(8,128)(2,1)S(1)} %get-tuple-element.78), channel_id=1, source_target_pairs={{0,32},{32,64},{64,96},{96,0},{1,33},{33,65},{65,97},{97,1},{2,34}... | collective-permute-start | bytes 393224 | tf_op jit(solution)/shard_map/ppermute | solution.py:412
  81.1 5.0 %collective-permute-start.19 = (bf16[256,256]{1,0:T(8,128)(2,1)S(1)}, bf16[256,256]{1,0:T(8,128)(2,1)S(1)}, u32[]{:S(2)}, u32[]{:S(2)}) collective-permute-start(bf16[256,256]{1,0:T(8,128)(2,1)S(1)} %get-tuple-element.80), channel_id=1, source_target_pairs={{0,96},{32,0},{64,32},{96,64},{1,97},{33,1},{65,33},{97,65},{2,98}... | collective-permute-start | bytes 393224 | tf_op jit(solution)/shard_map/ppermute | solution.py:412
  86.7 5.2 %collective-permute-start.20 = (bf16[64,256]{1,0:T(8,128)(2,1)S(1)}, bf16[64,256]{1,0:T(8,128)(2,1)S(1)}, u32[]{:S(2)}, u32[]{:S(2)}) collective-permute-start(bf16[64,256]{1,0:T(8,128)(2,1)S(1)} %get-tuple-element.86), channel_id=1, source_target_pairs={{0,4},{4,8},{8,12},{12,0},{1,5},{5,9},{9,13},{13,1},{2,6},{6,10},{... | collective-permute-start | bytes 98312 | tf_op jit(solution)/shard_map/ppermute | solution.py:412
  86.8 5.5 %collective-permute-start.21 = (bf16[64,256]{1,0:T(8,128)(2,1)S(1)}, bf16[64,256]{1,0:T(8,128)(2,1)S(1)}, u32[]{:S(2)}, u32[]{:S(2)}) collective-permute-start(bf16[64,256]{1,0:T(8,128)(2,1)S(1)} %get-tuple-element.87), channel_id=1, source_target_pairs={{0,8},{4,12},{8,0},{12,4},{1,9},{5,13},{9,1},{13,5},{2,10},{6,14},... | collective-permute-start | bytes 98312 | tf_op jit(solution)/shard_map/ppermute | solution.py:412
  88.9 4.3 %collective-permute-start.22 = (bf16[64,256]{1,0:T(8,128)(2,1)S(1)}, bf16[64,256]{1,0:T(8,128)(2,1)S(1)}, u32[]{:S(2)}, u32[]{:S(2)}) collective-permute-start(bf16[64,256]{1,0:T(8,128)(2,1)S(1)} %get-tuple-element.88), channel_id=1, source_target_pairs={{0,12},{4,0},{8,4},{12,8},{1,13},{5,1},{9,5},{13,9},{2,14},{6,2},{... | collective-permute-start | bytes 98312 | tf_op jit(solution)/shard_map/ppermute | solution.py:412
  93.7 3.8 %collective-permute-start.23 = (bf16[64,128]{1,0:T(8,128)(2,1)S(1)}, bf16[64,128]{1,0:T(8,128)(2,1)S(1)}, u32[]{:S(2)}, u32[]{:S(2)}) collective-permute-start(bf16[64,128]{1,0:T(8,128)(2,1)S(1)} %get-tuple-element.90), channel_id=1, source_target_pairs={{0,16},{16,0},{1,17},{17,1},{2,18},{18,2},{3,19},{19,3},{4,20},{20... | collective-permute-start | bytes 49160 | tf_op jit(solution)/shard_map/ppermute | solution.py:424
